TPU v7x, 256 devices: a whole 4x4x8 slice. The times are simulated.
256 devices in a mesh: group: 8 (over z), shard: 32 (over x, y, core).
Axes of the slice: x: 4, y: 4, z: 8, core: 2. Of those that a mesh axis runs over, the one named last changes fastest.
Arguments:
- gradient: float32 [37748736], P(('group', 'shard')), may hold values from -3000 to 3000
- momentum: float32 [37748736], P(('group', 'shard')), may hold values from -6 to 6
- master_weights: float32 [37748736], P(('group', 'shard')), may hold values from -0.3125 to 0.3125
- slot_table: int32 [24], replicated, may hold values from 0 to 23, as said below
Outputs:
- new_momentum: float32 [37748736], P(('group', 'shard'))
- update: float32 [37748736], P(('group', 'shard'))
- new_master: float32 [37748736], P(('group', 'shard'))
- weights: bfloat16 [37748736], P('group')
Inputs may be any that keep to these rules, and one draw needn't show every extreme that they name: `slot_table`: each of 0 to 23 appears exactly once.
All inputs are finite; a program needn't handle non-finite values.
Results may differ from a plain program's by a relative error of at most 0.0066.
Values may be sent and summed in bfloat16 or wider, within the bound.
No kernel may reach another device: no remote copies, remote signals or barrier semaphores. Data moves between devices by JAX's collectives and lax.ppermute only.
A program may use at most 64 MiB of HBM per device.

v0:
```python
import math

import jax
import jax.numpy as jnp
from jax import lax
from jax.experimental import pallas as pl
from jax.experimental.pallas import tpu as pltpu
from jax.sharding import PartitionSpec as P

D = 2048
FF = 768
MATS = 3
UNITS = 32
SHARD_TILES = 72
SHARD_ROWS = 1152
MAT_ROWS = 12288
MAT_TILES = 768
WIDE = 256

coef_first = 3.4445
coef_second = -4.775
coef_third = 2.0315
beta_momentum = 0.95
learn_rate = 0.02
weight_decay = 0.1

f32 = jnp.float32
bf16 = jnp.bfloat16
MIB = 2**20

VM = pl.BlockSpec(memory_space=pltpu.VMEM)
SM = pl.BlockSpec(memory_space=pltpu.SMEM)
ANY = pl.BlockSpec(memory_space=pl.ANY)
HBM = pl.BlockSpec(memory_space=pltpu.HBM)


def shard_of(x, y, c):
    return (x % 4) * 8 + (y % 4) * 2 + c


def first_route(step):
    route = []
    for x in range(4):
        for y in range(4):
            route.append((shard_of(x, y, 0), shard_of(x, y + step, 0)))
            route.append((shard_of(x, y, 1), shard_of(x + step, y, 1)))
    return route


def second_route(step):
    route = []
    for x in range(4):
        for y in range(4):
            route.append((shard_of(x, y, 0), shard_of(x + step, y, 0)))
            route.append((shard_of(x, y, 1), shard_of(x, y + step, 1)))
    return route


def swap_route():
    return [(s, s ^ 1) for s in range(32)]


def kind_of(info, matrix):
    kind = jnp.int32(0)
    for m in range(24):
        kind = jnp.where(info[m] == matrix, jnp.int32(m % 3), kind)
    return kind


def opening_kernel(g_in, master_in, sums_ref, narrow_ref, g_ref, master_ref, sems):
    half = SHARD_ROWS // 2
    loads = []
    for i, (source, target) in enumerate(((g_in, g_ref), (master_in, master_ref))):
        for n in range(2):
            rows = pl.ds(half * n, half)
            copy = pltpu.make_async_copy(source.at[rows, :], target.at[rows, :], sems.at[2 * i + n])
            copy.start()
            loads.append(copy)
    total = jnp.zeros((8, 128), f32)
    for n in range(2):
        loads[n].wait()
        gradient = g_ref[half * n : half * n + half, :]
        total = total + jnp.sum((gradient * gradient).reshape(half // 8, 8, 128), axis=0)
    total = jnp.sum(jnp.sum(total, axis=0, keepdims=True), axis=1, keepdims=True)
    sums_ref[...] = jnp.broadcast_to(total, (32, 128))
    for n in range(2):
        loads[2 + n].wait()
        rows = slice(half * n, half * n + half)
        narrow_ref[rows, :] = master_ref[rows, :].astype(bf16)


def join_kernel(*refs):
    for out, taken in zip(refs[4:], (refs[:4], refs[:2], refs[2:4])):
        length = taken[0].shape[0]
        for i, ref in enumerate(taken):
            out[length * i : length * i + length] = ref[...]


def look_kernel(info, sums, g_ref, m_ref, nm_ref, look_ref, scratch):
    total = jnp.sum(sums[...], axis=0, keepdims=True)[:, :1]
    clip = jnp.minimum(1.0, 0.5 * math.sqrt(24 * D * FF) / jnp.sqrt(total + 1e-06))
    clipped = clip * g_ref[...]
    new_momentum = beta_momentum * m_ref[...] + clipped
    nm_ref[...] = new_momentum
    scratch[...] = clipped + beta_momentum * new_momentum
    group, shard = info[24], info[25]
    for t in range(3):
        kind = kind_of(info, 3 * group + (3 * shard + t) // UNITS)
        row = 384 * t

        @pl.when(kind != 2)
        def _():
            for a in range(4):
                for j in range(6):
                    tile = scratch[pl.ds(row + 96 * a + j, 16, stride=6), :]
                    look_ref[24 * t + 6 * a + j] = tile.astype(bf16)

        @pl.when(kind == 2)
        def _():
            for j in range(16):
                tile = scratch[pl.ds(row + j, 16, stride=16), :]
                look_ref[24 * t + j] = tile.astype(bf16)
            for q in range(8):
                low = scratch[pl.ds(row + 256 + q, 8, stride=16), :]
                high = scratch[pl.ds(row + 264 + q, 8, stride=16), :]
                look_ref[24 * t + 16 + q] = jnp.concatenate([low, high], 0).astype(bf16)


def tiles(x, first, count, stride):
    return jnp.concatenate([x[first + stride * i] for i in range(count)], 0)


def mm(a, b):
    return jnp.dot(a, b, preferred_element_type=f32)


def mm_t(a, b):
    return lax.dot_general(a, b, (((1,), (1,)), ((), ())), preferred_element_type=f32)


def orthogonalize(kind, base, x, wide, flat, a0, b0, wb, b1, total, emit):
    @pl.when(kind == 2)
    def _():
        def pair(i, carry):
            t = base + 48 * i
            for h in range(2):
                rows = pl.ds(pl.multiple_of(32 * i + 16 * h, 16), 16)
                for j in range(16):
                    wide[rows, 128 * j : 128 * j + 128] = x[t + 24 * h + j]
            rows = pl.ds(pl.multiple_of(512 + 16 * i, 16), 16)
            for q in range(8):
                one = x[t + 16 + q].astype(f32)
                two = x[t + 40 + q].astype(f32)
                low = jnp.concatenate([one[:8], two[:8]], 0).astype(bf16)
                high = jnp.concatenate([one[8:], two[8:]], 0).astype(bf16)
                wide[rows, 128 * q : 128 * q + 128] = low
                wide[rows, 128 * (q + 8) : 128 * (q + 8) + 128] = high
            return carry

        lax.fori_loop(0, 16, pair, 0)

    @pl.when(kind != 2)
    def _():
        def chunk(i, carry):
            columns = pl.ds(pl.multiple_of(WIDE * i, WIDE), WIDE)
            for j in range(6):
                wide[128 * j : 128 * j + 128, columns] = tiles(x, base + 96 * i + j, 16, 6).T
            return carry

        lax.fori_loop(0, 8, chunk, 0)

    parts = [slice(WIDE * n, WIDE * n + WIDE) for n in range(3)]
    lower = [slice(WIDE * n, FF) for n in range(3)]
    iota = lax.broadcasted_iota

    def mirror(target, n):
        for m in range(n + 1, 3):
            target[parts[n], parts[m]] = target[parts[m], parts[n]].T

    square_sum = jnp.zeros((1, 1), f32)
    same = iota(jnp.int32, (WIDE, WIDE), 0) == iota(jnp.int32, (WIDE, WIDE), 1)
    for n, part in enumerate(parts):
        total[lower[n], part] = mm_t(wide[lower[n], :], wide[part, :])
        square_sum = square_sum + jnp.sum(jnp.where(same, total[part, part], 0.0), keepdims=True)
    inverse = 1.0 / (jnp.sqrt(square_sum) + 1e-07)
    for n, part in enumerate(parts):
        a0[lower[n], part] = (total[lower[n], part] * inverse * inverse).astype(bf16)
        mirror(a0, n)
    for n, part in enumerate(parts):
        square = mm(a0[lower[n], :], a0[:, part])
        poly = coef_second * a0[lower[n], part].astype(f32) + coef_third * square
        b0[lower[n], part] = poly.astype(bf16)
        mirror(b0, n)
    for n, part in enumerate(parts):
        step = coef_first * a0[lower[n], part].astype(f32) + mm(a0[lower[n], :], b0[:, part])
        total[lower[n], part] = coef_first * step
        wb[lower[n], part] = step.astype(bf16)
        mirror(wb, n)
    a1 = a0
    for n, part in enumerate(parts):
        step = total[lower[n], part] + mm(b0[lower[n], :], wb[:, part])
        a1[lower[n], part] = step.astype(bf16)
        mirror(a1, n)
    for n, part in enumerate(parts):
        square = mm(a1[lower[n], :], a1[:, part])
        poly = coef_second * a1[lower[n], part].astype(f32) + coef_third * square
        b1[lower[n], part] = poly.astype(bf16)
        mirror(b1, n)
    scale = inverse
    rest = wb
    diagonal_row = []
    diagonal_column = []
    for n, part in enumerate(parts):
        both = b0[lower[n], part].astype(f32) + b1[lower[n], part].astype(f32)
        step = coef_first * both + mm(b1[lower[n], :], b0[:, part])
        top = jnp.where(same, step[:WIDE], 0.0)
        diagonal_row.append(jnp.sum(top, axis=0, keepdims=True))
        diagonal_column.append(jnp.sum(top, axis=1, keepdims=True))
        rest[part, part] = jnp.where(same, 0.0, step[:WIDE]).astype(bf16)
        if n < 2:
            rest[lower[n + 1], part] = step[WIDE:].astype(bf16)
        mirror(rest, n)
    diagonal_column = jnp.concatenate(diagonal_column, 0)
    diagonal_row = (jnp.concatenate(diagonal_row, 1) + coef_first * coef_first) * scale
    diagonal_column = (diagonal_column + coef_first * coef_first) * scale

    @pl.when(kind != 2)
    def _():
        def chunk(i, carry):
            block = jnp.concatenate([tiles(x, base + 192 * i + j, 32, 6) for j in range(6)], 1)
            moved = mm(block, rest[...]) * scale + block.astype(f32) * diagonal_row
            for j in range(6):
                rows = pl.ds(3072 * i + j, 2 * WIDE, stride=6)
                flat[rows, :] = moved[:, 128 * j : 128 * j + 128]
            emit(2 * i)
            emit(2 * i + 1)
            return carry

        lax.fori_loop(0, 4, chunk, 0)

    @pl.when(kind == 2)
    def _():
        def chunk(i, carry):
            block = wide[:, pl.ds(pl.multiple_of(WIDE * i, WIDE), WIDE)]
            moved = mm(rest[...], block) * scale + block.astype(f32) * diagonal_column
            for h in range(2):
                panel = moved[:, 128 * h : 128 * h + 128]
                start = 2 * i + h
                for u in range(UNITS):
                    rows = pl.ds(start + 384 * u, 16, stride=16)
                    flat[rows, :] = panel[16 * u : 16 * u + 16]
                    rows = pl.ds(start + 384 * u + 256, 8, stride=16)
                    flat[rows, :] = panel[512 + 8 * u : 512 + 8 * u + 8]
            return carry

        lax.fori_loop(0, 8, chunk, 0)

        def emit_one(i, carry):
            emit(i)
            return carry

        lax.fori_loop(0, 8, emit_one, 0)


def held_table(shard):
    n = jnp.arange(32, dtype=jnp.int32)
    partner, hops = n // 16, n % 4
    second = (n // 4) % 4
    second = jnp.where(second < 2, second, 5 - second)
    row, column, core = shard // 8, (shard // 2) % 4, shard % 2
    holder = core + partner - 2 * core * partner
    at_zero = shard_of(row - second + 4, column - hops + 4, 0)
    at_one = shard_of(row - hops + 4, column - second + 4, 1)
    return jnp.where(holder == 0, at_zero, at_one)


def held(info, partner, second, hops):
    return info[26 + 16 * int(partner) + 4 * HOPS.index(second) + hops]


def arrivals(info, sources, slots):
    found = []
    for source, (partner, second, first_hops) in zip(sources, slots):
        for slot, hops in enumerate(first_hops):
            found.append((source, slot, held(info, partner, second, hops)))
    return found


def matrix_kernel(last, *refs):
    info, sources, refs = refs[0], refs[1:15], refs[15:]
    result, x, wide, flat, a0, b0, wb, b1, total, out_block, sems, more = refs
    group, shard = info[24], info[25]
    matrix = jnp.int32(2) if last else shard % 2
    first = (UNITS * matrix) // 3
    final = (UNITS * matrix + UNITS - 1) // 3
    loads = []
    for i, (source, slot, place) in enumerate(arrivals(info, sources, BLOCKS)):
        wanted = (place >= first) & (place <= final)
        target = SHARD_TILES * jnp.clip(place - first, 0, 11)
        copy = pltpu.make_async_copy(
            source.at[pl.ds(SHARD_TILES * slot, SHARD_TILES)],
            x.at[pl.ds(target, SHARD_TILES)],
            sems.at[i],
        )
        loads.append((wanted, copy))
    for wanted, copy in loads:
        pl.when(wanted)(copy.start)
    for wanted, copy in loads:
        pl.when(wanted)(copy.wait)

    kind = kind_of(info, 3 * group + matrix)
    base = MAT_TILES * matrix - SHARD_TILES * first

    def store(i):
        rows = pl.ds(pl.multiple_of(1536 * i, 1536), 1536)
        return pltpu.make_async_copy(out_block.at[rows, :], result.at[rows, :], more.at[i])

    def emit(i):
        rows = pl.ds(pl.multiple_of(1536 * i, 1536), 1536)
        out_block[rows, :] = flat[rows, :].astype(bf16)
        store(i).start()

    orthogonalize(kind, base, x, wide, flat, a0, b0, wb, b1, total, emit)
    for i in range(8):
        store(i).wait()


HOPS = (0, 1, 3, 2)
BLOCKS = [
    (p, q, dp)
    for p in (False, True)
    for q, dp in ((0, (0, 1, 2, 3)), (1, (0, 1)), (3, (2, 3)), (1, (2, 3)), (3, (0, 1)))
]
BLOCKS = BLOCKS[:5] + [(False, 2, (0, 1)), (False, 2, (2, 3))] + BLOCKS[5:]
BLOCKS = BLOCKS + [(True, 2, (0, 1)), (True, 2, (2, 3))]
QUADS = [(p, q, (0, 1, 2, 3)) for p in (False, True) for q in HOPS]


MATRIX_SCRATCH = [
    pltpu.VMEM((12 * SHARD_TILES, 16, 128), bf16),
    pltpu.VMEM((FF, D), bf16),
    pltpu.VMEM((MAT_ROWS, 128), f32),
    pltpu.VMEM((FF, FF), bf16),
    pltpu.VMEM((FF, FF), bf16),
    pltpu.VMEM((FF, FF), bf16),
    pltpu.VMEM((FF, FF), bf16),
    pltpu.VMEM((FF, FF), f32),
    pltpu.VMEM((MAT_ROWS, 128), bf16),
    pltpu.SemaphoreType.DMA((32,)),
    pltpu.SemaphoreType.DMA((8,)),
]


KEEP = 1.0 - learn_rate * weight_decay
RATE = learn_rate * 0.2 * math.sqrt(D)


def finish_kernel(info, *refs):
    mine, theirs, third, master_ref = refs[:4]
    sources = refs[4:11]
    weights, update_ref, new_ref, rest_ref, moves, results, sems, stores = refs[11:]
    shard = info[25]
    core = shard % 2
    loads = []
    for i, (source, matrix) in enumerate(((mine, core), (theirs, 1 - core), (third, 2))):
        rows = pl.ds(pl.multiple_of(MAT_ROWS * matrix, MAT_ROWS), MAT_ROWS)
        copy = pltpu.make_async_copy(source, moves.at[rows, :], sems.at[i])
        copy.start()
        loads.append(copy)
    for copy in loads:
        copy.wait()

    def rows_of(place):
        return pl.ds(pl.multiple_of(SHARD_ROWS * place, SHARD_ROWS), SHARD_ROWS)

    def store(place, i):
        rows = rows_of(place)
        return pltpu.make_async_copy(results.at[rows, :], weights.at[rows, :], stores.at[i])

    for i, (source, (partner, second, _)) in enumerate(zip(sources, QUADS)):

        def weigh(slot, carry):
            place = held(info, partner, second, slot)
            rows = rows_of(place)
            kept = source[rows_of(slot), :].astype(f32) * KEEP
            results[rows, :] = (kept - RATE * moves[rows, :].astype(f32)).astype(bf16)
            store(place, 4 * i + slot).start()
            return carry

        lax.fori_loop(0, 4, weigh, 0)

    for _, slot, place in arrivals(info, [None], QUADS[7:]):
        rest_ref[SHARD_ROWS * slot : SHARD_ROWS * slot + SHARD_ROWS, :] = moves[rows_of(place), :]
    update = math.sqrt(D) * moves[rows_of(shard), :].astype(f32)
    update_ref[...] = update
    new_ref[...] = master_ref[...] * KEEP - learn_rate * 0.2 * update
    for i, (_, slot, place) in enumerate(arrivals(info, sources, QUADS[:7])):
        store(place, i).wait()


def closing_kernel(info, _, rest, masters, weights, results, stores):
    written = []
    for i, (_, _, place) in enumerate(arrivals(info, [None], QUADS[7:])):
        part = slice(SHARD_ROWS * i, SHARD_ROWS * i + SHARD_ROWS)
        kept = masters[part, :].astype(f32) * KEEP
        results[part, :] = (kept - RATE * rest[part, :].astype(f32)).astype(bf16)
        rows = pl.ds(pl.multiple_of(SHARD_ROWS * place, SHARD_ROWS), SHARD_ROWS)
        copy = pltpu.make_async_copy(results.at[part, :], weights.at[rows, :], stores.at[i])
        copy.start()
        written.append(copy)
    for copy in written:
        copy.wait()


def params(mib):
    return pltpu.CompilerParams(vmem_limit_bytes=mib * MIB)


def joined(blocks, parts):
    lengths = [4 * blocks[0].shape[0]] + [2 * blocks[0].shape[0]] * (parts - 1)
    return pl.pallas_call(
        join_kernel,
        out_shape=tuple(jax.ShapeDtypeStruct((n,) + blocks[0].shape[1:], bf16) for n in lengths),
        in_specs=[VM] * 4,
        out_specs=(VM,) * parts,
        compiler_params=params(8),
    )(*blocks)


def on_device(gradient, momentum, master_weights, slot_table):
    group = lax.axis_index("group").astype(jnp.int32)
    shard = lax.axis_index("shard").astype(jnp.int32)
    info = jnp.concatenate([slot_table, jnp.stack([group, shard]), held_table(shard)])
    gradient = gradient.reshape(SHARD_ROWS, 128)
    momentum = momentum.reshape(SHARD_ROWS, 128)
    master_weights = master_weights.reshape(SHARD_ROWS, 128)

    def send(block, route):
        return lax.ppermute(block, "shard", route)

    sums, narrow = pl.pallas_call(
        opening_kernel,
        out_shape=(
            jax.ShapeDtypeStruct((32, 128), f32),
            jax.ShapeDtypeStruct((SHARD_ROWS, 128), bf16),
        ),
        in_specs=[HBM, HBM],
        out_specs=(VM, VM),
        scratch_shapes=[
            pltpu.VMEM((SHARD_ROWS, 128), f32),
            pltpu.VMEM((SHARD_ROWS, 128), f32),
            pltpu.SemaphoreType.DMA((4,)),
        ],
        compiler_params=params(60),
    )(gradient, master_weights)
    masters = [narrow] + [send(narrow, first_route(step)) for step in (1, 2, 3)]
    sums = lax.all_to_all(sums, "shard", 0, 0)
    sums = jnp.broadcast_to(jnp.sum(sums, axis=0, keepdims=True), (8, 128))
    (quad,) = joined(masters, 1)
    quad, sums = lax.optimization_barrier((quad, sums))
    sums = lax.all_to_all(sums, "group", 0, 0)

    flat_shape = jax.ShapeDtypeStruct((SHARD_ROWS, 128), f32)
    new_momentum, look = pl.pallas_call(
        look_kernel,
        out_shape=(flat_shape, jax.ShapeDtypeStruct((SHARD_TILES, 16, 128), bf16)),
        in_specs=[SM, VM, VM, VM],
        out_specs=(VM, VM),
        scratch_shapes=[pltpu.VMEM((SHARD_ROWS, 128), f32)],
        compiler_params=params(8),
    )(info, sums, gradient, momentum)

    whole, ahead, behind = joined([look] + [send(look, first_route(step)) for step in (1, 2, 3)], 3)
    forward = [send(ahead, second_route(1)), send(behind, second_route(1))]
    backward = [send(ahead, second_route(3)), send(behind, second_route(3))]
    across = [send(forward[0], second_route(1)), send(backward[1], second_route(3))]
    whole, forward[0] = lax.optimization_barrier((whole, forward[0]))
    early = [whole, forward[0], backward[1], forward[1], backward[0]]
    swapped = [send(block, swap_route()) for block in early]
    across, swapped = lax.optimization_barrier((across, swapped))
    sources = early + across + swapped + [send(block, swap_route()) for block in across]

    quad, sources = lax.optimization_barrier((quad, sources))
    masters = [quad, send(quad, second_route(1)), send(quad, second_route(3))]

    cost = pl.CostEstimate(flops=9_300_000_000, bytes_accessed=20_000_000, transcendentals=0)

    def orthogonalized(last):
        return pl.pallas_call(
            lambda *refs: matrix_kernel(last, *refs),
            out_shape=jax.ShapeDtypeStruct((MAT_ROWS, 128), bf16),
            in_specs=[SM] + [HBM] * 14,
            out_specs=VM if last else ANY,
            scratch_shapes=MATRIX_SCRATCH,
            compiler_params=params(29),
            cost_estimate=cost,
        )(info, *sources)

    mine = orthogonalized(False)
    mine, masters = lax.optimization_barrier((mine, masters))
    theirs = send(mine, swap_route())
    across = send(masters[1], second_route(1))
    masters = masters + [across] + [send(block, swap_route()) for block in masters]
    third = orthogonalized(True)
    third, across = lax.optimization_barrier((third, across))
    last = send(across, swap_route())
    weights_shape = jax.ShapeDtypeStruct((MATS * MAT_ROWS, 128), bf16)
    quad_shape = jax.ShapeDtypeStruct((4 * SHARD_ROWS, 128), bf16)
    weights, update, new_master, rest = pl.pallas_call(
        finish_kernel,
        out_shape=(weights_shape, flat_shape, flat_shape, quad_shape),
        in_specs=[SM] + [VM] * 11,
        out_specs=(ANY, VM, VM, VM),
        scratch_shapes=[
            pltpu.VMEM((MATS * MAT_ROWS, 128), bf16),
            pltpu.VMEM((MATS * MAT_ROWS, 128), bf16),
            pltpu.SemaphoreType.DMA((3,)),
            pltpu.SemaphoreType.DMA((28,)),
        ],
        compiler_params=params(24),
        cost_estimate=pl.CostEstimate(flops=10_000_000, bytes_accessed=28_000_000, transcendentals=0),
    )(info, mine, theirs, third, master_weights, *masters)
    weights = pl.pallas_call(
        closing_kernel,
        out_shape=weights_shape,
        in_specs=[SM, ANY, VM, VM],
        out_specs=ANY,
        scratch_shapes=[
            pltpu.VMEM((4 * SHARD_ROWS, 128), bf16),
            pltpu.SemaphoreType.DMA((4,)),
        ],
        input_output_aliases={1: 0},
        compiler_params=params(16),
    )(info, weights, rest, last)
    return (
        new_momentum.reshape(-1),
        update.reshape(-1),
        new_master.reshape(-1),
        weights.reshape(-1),
    )


def solution(mesh):
    in_specs = (P(("group", "shard")), P(("group", "shard")), P(("group", "shard")), P())
    out_specs = (P(("group", "shard")), P(("group", "shard")), P(("group", "shard")), P("group"))
    return jax.shard_map(
        on_device, mesh=mesh, in_specs=in_specs, out_specs=out_specs, check_vma=False
    )
```

profile of v0, /device:TPU:1, one launch (start us, length us, event | category | flops | bytes accessed | tf_op | source)
XLA Modules:
  0.0 128.1 jit_solution(17507108387154744733)
XLA Ops:
  0.6 2.0 %shard_map.75 = (f32[32,128]{1,0:T(8,128)}, bf16[1152,128]{1,0:T(8,128)(2,1)}) custom-call(f32[1152,128]{1,0:T(8,128)} %bitcast.14, f32[1152,128]{1,0:T(8,128)} %bitcast.16), custom_call_target="tpu_custom_call" | custom-call | tf_op jit(solution)/shard_map/pallas_call | solution.py:441
  2.6 2.1 %collective-permute-start = (bf16[1152,128]{1,0:T(8,128)(2,1)}, bf16[1152,128]{1,0:T(8,128)(2,1)S(1)}, u32[]{:S(2)}, u32[]{:S(2)}) collective-permute-start(bf16[1152,128]{1,0:T(8,128)(2,1)} %get-tuple-element.47.refs_0_), channel_id=1, source_target_pairs={{0,2},{1,9},{2,4},{3,11},{4,6},{5,13},{6,0},{7,15},{8,10},{9,17},{... | collective-permute-start | bytes 884744 | tf_op jit(solution)/shard_map/ppermute | solution.py:439
  4.8 2.5 %collective-permute-start.1 = (bf16[1152,128]{1,0:T(8,128)(2,1)}, bf16[1152,128]{1,0:T(8,128)(2,1)S(1)}, u32[]{:S(2)}, u32[]{:S(2)}) collective-permute-start(bf16[1152,128]{1,0:T(8,128)(2,1)} %get-tuple-element.47.refs_0_), channel_id=1, source_target_pairs={{0,4},{1,17},{2,6},{3,19},{4,0},{5,21},{6,2},{7,23},{8,12},{9,25},... | collective-permute-start | bytes 884744 | tf_op jit(solution)/shard_map/ppermute | solution.py:439
  7.2 1.2 collective-permute-start.2
  8.4 6.3 %all-to-all-start = ((f32[32,1,128]{2,1,0:T(1,128)}), f32[32,1,128]{2,1,0:T(1,128)S(1)}, u32[]{:S(2)}, u32[]{:S(2)}) async-start(f32[32,1,128]{2,1,0:T(1,128)} %bitcast.21), calls=%async_computation | async-start | bytes 32768 | tf_op jit(solution)/shard_map/all_to_all | solution.py:457
  14.7 6.8 %all-to-all-done = f32[32,1,128]{2,1,0:T(1,128)S(1)} async-done(((f32[32,1,128]{2,1,0:T(1,128)}), f32[32,1,128]{2,1,0:T(1,128)S(1)}, u32[]{:S(2)}, u32[]{:S(2)}) %all-to-all-start) | async-done | bytes 16416 | tf_op jit(solution)/shard_map/all_to_all | solution.py:457
  21.6 1.0 copy-done.3
  23.3 8.2 %all-to-all-start.1 = ((f32[8,1,128]{2,1,0:T(1,128)}), f32[8,1,128]{2,1,0:T(1,128)S(1)}, u32[]{:S(2)}, u32[]{:S(2)}) async-start(f32[8,1,128]{2,1,0:T(1,128)} %bitcast.6), calls=%async_computation.1 | async-start | bytes 8192 | tf_op jit(solution)/shard_map/all_to_all | solution.py:461
  31.6 6.4 %all-to-all-done.1 = f32[8,1,128]{2,1,0:T(1,128)S(1)} async-done(((f32[8,1,128]{2,1,0:T(1,128)}), f32[8,1,128]{2,1,0:T(1,128)S(1)}, u32[]{:S(2)}, u32[]{:S(2)}) %all-to-all-start.1) | async-done | bytes 4128 | tf_op jit(solution)/shard_map/all_to_all | solution.py:461
  38.0 1.9 %shard_map.77 = (f32[1152,128]{1,0:T(8,128)}, bf16[72,16,128]{2,1,0:T(8,128)(2,1)S(1)}) custom-call(s32[58]{0:T(128)S(1)} %pad_add_fusion.info.refs_0_, f32[8,128]{1,0:T(8,128)S(1)} %bitcast.19, f32[1152,128]{1,0:T(8,128)S(1)} %bitcast.15, f32[1152,128]{1,0:T(8,128)S(1)} %bitcast.18), custom_call_target="tpu_custom_call" | custom-call | tf_op jit(solution)/shard_map/pallas_call | solution.py:464
  40.1 1.7 %collective-permute-start.4 = (bf16[72,16,128]{2,1,0:T(8,128)(2,1)S(1)}, bf16[72,16,128]{2,1,0:T(8,128)(2,1)S(1)}, u32[]{:S(2)}, u32[]{:S(2)}) collective-permute-start(bf16[72,16,128]{2,1,0:T(8,128)(2,1)S(1)} %get-tuple-element.52.refs_0_), channel_id=1, source_target_pairs={{0,4},{1,17},{2,6},{3,19},{4,0},{5,21},{6,2},{7,23},{8,12},{9,25},... | collective-permute-start | bytes 884744 | tf_op jit(solution)/shard_map/ppermute | solution.py:439
  41.9 0.8 collective-permute-start.5
  42.7 7.3 %collective-permute-done.3.refs_1_ = bf16[72,16,128]{2,1,0:T(8,128)(2,1)S(1)} collective-permute-done((bf16[72,16,128]{2,1,0:T(8,128)(2,1)S(1)}, bf16[72,16,128]{2,1,0:T(8,128)(2,1)S(1)}, u32[]{:S(2)}, u32[]{:S(2)}) %collective-permute-start.3) | collective-permute-done | bytes 294944 | tf_op jit(solution)/shard_map/ppermute | solution.py:439
  51.2 2.4 %collective-permute-start.7 = (bf16[144,16,128]{2,1,0:T(8,128)(2,1)S(1)}, bf16[144,16,128]{2,1,0:T(8,128)(2,1)S(1)}, u32[]{:S(2)}, u32[]{:S(2)}) collective-permute-start(bf16[144,16,128]{2,1,0:T(8,128)(2,1)S(1)} %get-tuple-element.57), channel_id=1, source_target_pairs={{0,24},{1,7},{2,26},{3,1},{4,28},{5,3},{6,30},{7,5},{8,0},{9,15},{... | collective-permute-start | bytes 1769480 | tf_op jit(solution)/shard_map/ppermute | solution.py:439
  53.6 2.7 %collective-permute-start.9 = (bf16[144,16,128]{2,1,0:T(8,128)(2,1)S(1)}, bf16[144,16,128]{2,1,0:T(8,128)(2,1)S(1)}, u32[]{:S(2)}, u32[]{:S(2)}) collective-permute-start(bf16[144,16,128]{2,1,0:T(8,128)(2,1)S(1)} %get-tuple-element.54), channel_id=1, source_target_pairs={{0,24},{1,7},{2,26},{3,1},{4,28},{5,3},{6,30},{7,5},{8,0},{9,15},{... | collective-permute-start | bytes 1769480 | tf_op jit(solution)/shard_map/ppermute | solution.py:439
  56.3 4.9 %collective-permute-done.6.refs_2_ = bf16[144,16,128]{2,1,0:T(8,128)(2,1)S(1)} collective-permute-done((bf16[144,16,128]{2,1,0:T(8,128)(2,1)S(1)}, bf16[144,16,128]{2,1,0:T(8,128)(2,1)S(1)}, u32[]{:S(2)}, u32[]{:S(2)}) %collective-permute-start.6) | collective-permute-done | bytes 589856 | tf_op jit(solution)/shard_map/ppermute | solution.py:439
  61.2 2.7 %collective-permute-start.11 = (bf16[144,16,128]{2,1,0:T(8,128)(2,1)S(1)}, bf16[144,16,128]{2,1,0:T(8,128)(2,1)S(1)}, u32[]{:S(2)}, u32[]{:S(2)}) collective-permute-start(bf16[144,16,128]{2,1,0:T(8,128)(2,1)S(1)} %collective-permute-done.7.refs_3_), channel_id=1, source_target_pairs={{0,24},{1,7},{2,26},{3,1},{4,28},{5,3},{6,30},{7,5},{8,0},{9,15},{... | collective-permute-start | bytes 1769480 | tf_op jit(solution)/shard_map/ppermute | solution.py:439
  63.8 4.6 %collective-permute-start.12 = (bf16[288,16,128]{2,1,0:T(8,128)(2,1)S(1)}, bf16[288,16,128]{2,1,0:T(8,128)(2,1)S(1)}, u32[]{:S(2)}, u32[]{:S(2)}) collective-permute-start(bf16[288,16,128]{2,1,0:T(8,128)(2,1)S(1)} %get-tuple-element.65.refs_1_), channel_id=1, source_target_pairs={{0,1},{1,0},{2,3},{3,2},{4,5},{5,4},{6,7},{7,6},{8,9},{9,8},{10,11... | collective-permute-start | bytes 3538952 | tf_op jit(solution)/shard_map/ppermute | solution.py:439
  68.5 3.1 %collective-permute-start.13 = (bf16[144,16,128]{2,1,0:T(8,128)(2,1)S(1)}, bf16[144,16,128]{2,1,0:T(8,128)(2,1)S(1)}, u32[]{:S(2)}, u32[]{:S(2)}) collective-permute-start(bf16[144,16,128]{2,1,0:T(8,128)(2,1)S(1)} %collective-permute-done.6.refs_2_), channel_id=1, source_target_pairs={{0,1},{1,0},{2,3},{3,2},{4,5},{5,4},{6,7},{7,6},{8,9},{9,8},{10,11... | collective-permute-start | bytes 1769480 | tf_op jit(solution)/shard_map/ppermute | solution.py:439
  71.6 2.2 %collective-permute-done.10.refs_6_ = bf16[144,16,128]{2,1,0:T(8,128)(2,1)S(1)} collective-permute-done((bf16[144,16,128]{2,1,0:T(8,128)(2,1)S(1)}, bf16[144,16,128]{2,1,0:T(8,128)(2,1)S(1)}, u32[]{:S(2)}, u32[]{:S(2)}) %collective-permute-start.10) | collective-permute-done | bytes 589856 | tf_op jit(solution)/shard_map/ppermute | solution.py:439
  73.8 4.1 %collective-permute-start.15 = (bf16[144,16,128]{2,1,0:T(8,128)(2,1)S(1)}, bf16[144,16,128]{2,1,0:T(8,128)(2,1)S(1)}, u32[]{:S(2)}, u32[]{:S(2)}) collective-permute-start(bf16[144,16,128]{2,1,0:T(8,128)(2,1)S(1)} %collective-permute-done.8.refs_4_), channel_id=1, source_target_pairs={{0,1},{1,0},{2,3},{3,2},{4,5},{5,4},{6,7},{7,6},{8,9},{9,8},{10,11... | collective-permute-start | bytes 1769480 | tf_op jit(solution)/shard_map/ppermute | solution.py:439
  77.9 1.6 %collective-permute-done.15.refs_11_ = bf16[144,16,128]{2,1,0:T(8,128)(2,1)S(1)} collective-permute-done((bf16[144,16,128]{2,1,0:T(8,128)(2,1)S(1)}, bf16[144,16,128]{2,1,0:T(8,128)(2,1)S(1)}, u32[]{:S(2)}, u32[]{:S(2)}) %collective-permute-start.15) | collective-permute-done | bytes 589856 | tf_op jit(solution)/shard_map/ppermute | solution.py:439
  79.5 0.8 collective-permute-done.16.refs_12_
  80.9 1.5 %collective-permute-done.17.refs_13_ = bf16[144,16,128]{2,1,0:T(8,128)(2,1)S(1)} collective-permute-done((bf16[144,16,128]{2,1,0:T(8,128)(2,1)S(1)}, bf16[144,16,128]{2,1,0:T(8,128)(2,1)S(1)}, u32[]{:S(2)}, u32[]{:S(2)}) %collective-permute-start.17) | collective-permute-done | bytes 589856 | tf_op jit(solution)/shard_map/ppermute | solution.py:439
  82.3 0.8 collective-permute-done.18.refs_14_
  83.4 2.4 %collective-permute-start.20 = (bf16[4608,128]{1,0:T(8,128)(2,1)S(1)}, bf16[4608,128]{1,0:T(8,128)(2,1)S(1)}, u32[]{:S(2)}, u32[]{:S(2)}) collective-permute-start(bf16[4608,128]{1,0:T(8,128)(2,1)S(1)} %shard_map.76.refs_4_), channel_id=1, source_target_pairs={{0,24},{1,7},{2,26},{3,1},{4,28},{5,3},{6,30},{7,5},{8,0},{9,15},{... | collective-permute-start | bytes 3538952 | tf_op jit(solution)/shard_map/ppermute | solution.py:439
  85.9 14.2 %shard_map.79.refs_0_ = bf16[12288,128]{1,0:T(8,128)(2,1)S(1)} custom-call(s32[58]{0:T(128)S(1)} %pad_add_fusion.info.refs_0_, bf16[288,16,128]{2,1,0:T(8,128)(2,1)S(1)} %get-tuple-element.65.refs_1_, bf16[144,16,128]{2,1,0:T(8,128)(2,1)S(1)} %collective-permute-done.6.refs_2_, bf16[144,16,128]{2,1,0:T(8,128)(2,1)S(1)} %collective-permute-done.7.refs_3_, ...), custom_call_target="tpu_custom_call" | custom-call | flops 9299999744 | bytes 20000000 | tf_op jit(solution)/shard_map/pallas_call | solution.py:489
  100.1 2.0 %collective-permute-start.21 = (bf16[12288,128]{1,0:T(8,128)(2,1)S(1)}, bf16[12288,128]{1,0:T(8,128)(2,1)S(1)}, u32[]{:S(2)}, u32[]{:S(2)}) collective-permute-start(bf16[12288,128]{1,0:T(8,128)(2,1)S(1)} %shard_map.79.refs_0_), channel_id=1, source_target_pairs={{0,1},{1,0},{2,3},{3,2},{4,5},{5,4},{6,7},{7,6},{8,9},{9,8},{10,11... | collective-permute-start | bytes 9437192 | tf_op jit(solution)/shard_map/ppermute | solution.py:439
  103.0 15.2 %shard_map.80.refs_2_ = bf16[12288,128]{1,0:T(8,128)(2,1)S(1)} custom-call(s32[58]{0:T(128)S(1)} %pad_add_fusion.info.refs_0_, bf16[288,16,128]{2,1,0:T(8,128)(2,1)S(1)} %get-tuple-element.65.refs_1_, bf16[144,16,128]{2,1,0:T(8,128)(2,1)S(1)} %collective-permute-done.6.refs_2_, bf16[144,16,128]{2,1,0:T(8,128)(2,1)S(1)} %collective-permute-done.7.refs_3_, ...), custom_call_target="tpu_custom_call" | custom-call | flops 9299999744 | bytes 20000000 | tf_op jit(solution)/shard_map/pallas_call | solution.py:489
  118.7 1.2 collective-permute-start.26
  119.9 6.3 %shard_map.81 = (bf16[36864,128]{1,0:T(8,128)(2,1)}, f32[1152,128]{1,0:T(8,128)}, f32[1152,128]{1,0:T(8,128)}, bf16[4608,128]{1,0:T(8,128)(2,1)S(1)}) custom-call(s32[58]{0:T(128)S(1)} %pad_add_fusion.info.refs_0_, bf16[12288,128]{1,0:T(8,128)(2,1)S(1)} %shard_map.79.refs_0_, bf16[12288,128]{1,0:T(8,128)(2,1)S(1)} %collective-permute-done.21.refs_1_, ...), custom_call_target="tpu_custom_call" | custom-call | flops 10000000 | bytes 28000000 | tf_op jit(solution)/shard_map/pallas_call | solution.py:509
  126.2 1.7 %shard_map.82 = bf16[36864,128]{1,0:T(8,128)(2,1)} custom-call(s32[58]{0:T(128)S(1)} %pad_add_fusion.info.refs_0_, bf16[36864,128]{1,0:T(8,128)(2,1)} %get-tuple-element.87._, bf16[4608,128]{1,0:T(8,128)(2,1)S(1)} %get-tuple-element.88.rest, bf16[4608,128]{1,0:T(8,128)(2,1)S(1)} %collective-permute-done.26.masters), custom_call_target="tpu_custom_call", output_to_operand_aliasing={{}: (1, {})} | custom-call | tf_op jit(solution)/shard_map/pallas_call | solution.py:523
  (48 shorter events, 4.5 us)
Async XLA Ops:
  2.6 18.9 %collective-permute-start = (bf16[1152,128]{1,0:T(8,128)(2,1)}, bf16[1152,128]{1,0:T(8,128)(2,1)S(1)}, u32[]{:S(2)}, u32[]{:S(2)}) collective-permute-start(bf16[1152,128]{1,0:T(8,128)(2,1)} %get-tuple-element.47.refs_0_), channel_id=1, source_target_pairs={{0,2},{1,9},{2,4},{3,11},{4,6},{5,13},{6,0},{7,15},{8,10},{9,17},{... | collective-permute-start | bytes 884744 | tf_op jit(solution)/shard_map/ppermute | solution.py:439
  4.8 16.8 %collective-permute-start.1 = (bf16[1152,128]{1,0:T(8,128)(2,1)}, bf16[1152,128]{1,0:T(8,128)(2,1)S(1)}, u32[]{:S(2)}, u32[]{:S(2)}) collective-permute-start(bf16[1152,128]{1,0:T(8,128)(2,1)} %get-tuple-element.47.refs_0_), channel_id=1, source_target_pairs={{0,4},{1,17},{2,6},{3,19},{4,0},{5,21},{6,2},{7,23},{8,12},{9,25},... | collective-permute-start | bytes 884744 | tf_op jit(solution)/shard_map/ppermute | solution.py:439
  7.2 14.4 %collective-permute-start.2 = (bf16[1152,128]{1,0:T(8,128)(2,1)}, bf16[1152,128]{1,0:T(8,128)(2,1)S(1)}, u32[]{:S(2)}, u32[]{:S(2)}) collective-permute-start(bf16[1152,128]{1,0:T(8,128)(2,1)} %get-tuple-element.47.refs_0_), channel_id=1, source_target_pairs={{0,6},{1,25},{2,0},{3,27},{4,2},{5,29},{6,4},{7,31},{8,14},{9,1},{... | collective-permute-start | bytes 884744 | tf_op jit(solution)/shard_map/ppermute | solution.py:439
  8.4 13.1 %all-to-all-start = ((f32[32,1,128]{2,1,0:T(1,128)}), f32[32,1,128]{2,1,0:T(1,128)S(1)}, u32[]{:S(2)}, u32[]{:S(2)}) async-start(f32[32,1,128]{2,1,0:T(1,128)} %bitcast.21), calls=%async_computation | async-start | bytes 32768 | tf_op jit(solution)/shard_map/all_to_all | solution.py:457
  21.5 16.4 %copy-start = (f32[147456]{0:T(1024)S(1)}, f32[147456]{0:T(1024)}, u32[]{:S(2)}) copy-start(f32[147456]{0:T(1024)} %param.4) | copy-start | bytes 1769476
  21.5 16.4 %copy-start.2 = (f32[147456]{0:T(1024)S(1)}, f32[147456]{0:T(1024)}, u32[]{:S(2)}) copy-start(f32[147456]{0:T(1024)} %param.5) | copy-start | bytes 1769476
  23.3 14.6 %all-to-all-start.1 = ((f32[8,1,128]{2,1,0:T(1,128)}), f32[8,1,128]{2,1,0:T(1,128)S(1)}, u32[]{:S(2)}, u32[]{:S(2)}) async-start(f32[8,1,128]{2,1,0:T(1,128)} %bitcast.6), calls=%async_computation.1 | async-start | bytes 8192 | tf_op jit(solution)/shard_map/all_to_all | solution.py:461
  39.8 10.2 %collective-permute-start.3 = (bf16[72,16,128]{2,1,0:T(8,128)(2,1)S(1)}, bf16[72,16,128]{2,1,0:T(8,128)(2,1)S(1)}, u32[]{:S(2)}, u32[]{:S(2)}) collective-permute-start(bf16[72,16,128]{2,1,0:T(8,128)(2,1)S(1)} %get-tuple-element.52.refs_0_), channel_id=1, source_target_pairs={{0,2},{1,9},{2,4},{3,11},{4,6},{5,13},{6,0},{7,15},{8,10},{9,17},{... | collective-permute-start | bytes 884744 | tf_op jit(solution)/shard_map/ppermute | solution.py:439
  40.1 9.9 %collective-permute-start.4 = (bf16[72,16,128]{2,1,0:T(8,128)(2,1)S(1)}, bf16[72,16,128]{2,1,0:T(8,128)(2,1)S(1)}, u32[]{:S(2)}, u32[]{:S(2)}) collective-permute-start(bf16[72,16,128]{2,1,0:T(8,128)(2,1)S(1)} %get-tuple-element.52.refs_0_), channel_id=1, source_target_pairs={{0,4},{1,17},{2,6},{3,19},{4,0},{5,21},{6,2},{7,23},{8,12},{9,25},... | collective-permute-start | bytes 884744 | tf_op jit(solution)/shard_map/ppermute | solution.py:439
  41.9 8.8 %collective-permute-start.5 = (bf16[72,16,128]{2,1,0:T(8,128)(2,1)S(1)}, bf16[72,16,128]{2,1,0:T(8,128)(2,1)S(1)}, u32[]{:S(2)}, u32[]{:S(2)}) collective-permute-start(bf16[72,16,128]{2,1,0:T(8,128)(2,1)S(1)} %get-tuple-element.52.refs_0_), channel_id=1, source_target_pairs={{0,6},{1,25},{2,0},{3,27},{4,2},{5,29},{6,4},{7,31},{8,14},{9,1},{... | collective-permute-start | bytes 884744 | tf_op jit(solution)/shard_map/ppermute | solution.py:439
  50.8 10.3 %collective-permute-start.6 = (bf16[144,16,128]{2,1,0:T(8,128)(2,1)S(1)}, bf16[144,16,128]{2,1,0:T(8,128)(2,1)S(1)}, u32[]{:S(2)}, u32[]{:S(2)}) collective-permute-start(bf16[144,16,128]{2,1,0:T(8,128)(2,1)S(1)} %get-tuple-element.54), channel_id=1, source_target_pairs={{0,8},{1,3},{2,10},{3,5},{4,12},{5,7},{6,14},{7,1},{8,16},{9,11},{... | collective-permute-start | bytes 1769480 | tf_op jit(solution)/shard_map/ppermute | solution.py:439
  51.2 10.0 %collective-permute-start.7 = (bf16[144,16,128]{2,1,0:T(8,128)(2,1)S(1)}, bf16[144,16,128]{2,1,0:T(8,128)(2,1)S(1)}, u32[]{:S(2)}, u32[]{:S(2)}) collective-permute-start(bf16[144,16,128]{2,1,0:T(8,128)(2,1)S(1)} %get-tuple-element.57), channel_id=1, source_target_pairs={{0,24},{1,7},{2,26},{3,1},{4,28},{5,3},{6,30},{7,5},{8,0},{9,15},{... | collective-permute-start | bytes 1769480 | tf_op jit(solution)/shard_map/ppermute | solution.py:439
  53.6 14.9 %collective-permute-start.8 = (bf16[144,16,128]{2,1,0:T(8,128)(2,1)S(1)}, bf16[144,16,128]{2,1,0:T(8,128)(2,1)S(1)}, u32[]{:S(2)}, u32[]{:S(2)}) collective-permute-start(bf16[144,16,128]{2,1,0:T(8,128)(2,1)S(1)} %get-tuple-element.57), channel_id=1, source_target_pairs={{0,8},{1,3},{2,10},{3,5},{4,12},{5,7},{6,14},{7,1},{8,16},{9,11},{... | collective-permute-start | bytes 1769480 | tf_op jit(solution)/shard_map/ppermute | solution.py:439
  53.6 18.0 %collective-permute-start.9 = (bf16[144,16,128]{2,1,0:T(8,128)(2,1)S(1)}, bf16[144,16,128]{2,1,0:T(8,128)(2,1)S(1)}, u32[]{:S(2)}, u32[]{:S(2)}) collective-permute-start(bf16[144,16,128]{2,1,0:T(8,128)(2,1)S(1)} %get-tuple-element.54), channel_id=1, source_target_pairs={{0,24},{1,7},{2,26},{3,1},{4,28},{5,3},{6,30},{7,5},{8,0},{9,15},{... | collective-permute-start | bytes 1769480 | tf_op jit(solution)/shard_map/ppermute | solution.py:439
  61.2 12.6 %collective-permute-start.10 = (bf16[144,16,128]{2,1,0:T(8,128)(2,1)S(1)}, bf16[144,16,128]{2,1,0:T(8,128)(2,1)S(1)}, u32[]{:S(2)}, u32[]{:S(2)}) collective-permute-start(bf16[144,16,128]{2,1,0:T(8,128)(2,1)S(1)} %collective-permute-done.6.refs_2_), channel_id=1, source_target_pairs={{0,8},{1,3},{2,10},{3,5},{4,12},{5,7},{6,14},{7,1},{8,16},{9,11},{... | collective-permute-start | bytes 1769480 | tf_op jit(solution)/shard_map/ppermute | solution.py:439
  61.2 16.7 %collective-permute-start.11 = (bf16[144,16,128]{2,1,0:T(8,128)(2,1)S(1)}, bf16[144,16,128]{2,1,0:T(8,128)(2,1)S(1)}, u32[]{:S(2)}, u32[]{:S(2)}) collective-permute-start(bf16[144,16,128]{2,1,0:T(8,128)(2,1)S(1)} %collective-permute-done.7.refs_3_), channel_id=1, source_target_pairs={{0,24},{1,7},{2,26},{3,1},{4,28},{5,3},{6,30},{7,5},{8,0},{9,15},{... | collective-permute-start | bytes 1769480 | tf_op jit(solution)/shard_map/ppermute | solution.py:439
  63.8 16.5 %collective-permute-start.12 = (bf16[288,16,128]{2,1,0:T(8,128)(2,1)S(1)}, bf16[288,16,128]{2,1,0:T(8,128)(2,1)S(1)}, u32[]{:S(2)}, u32[]{:S(2)}) collective-permute-start(bf16[288,16,128]{2,1,0:T(8,128)(2,1)S(1)} %get-tuple-element.65.refs_1_), channel_id=1, source_target_pairs={{0,1},{1,0},{2,3},{3,2},{4,5},{5,4},{6,7},{7,6},{8,9},{9,8},{10,11... | collective-permute-start | bytes 3538952 | tf_op jit(solution)/shard_map/ppermute | solution.py:439
  68.5 9.4 %collective-permute-start.13 = (bf16[144,16,128]{2,1,0:T(8,128)(2,1)S(1)}, bf16[144,16,128]{2,1,0:T(8,128)(2,1)S(1)}, u32[]{:S(2)}, u32[]{:S(2)}) collective-permute-start(bf16[144,16,128]{2,1,0:T(8,128)(2,1)S(1)} %collective-permute-done.6.refs_2_), channel_id=1, source_target_pairs={{0,1},{1,0},{2,3},{3,2},{4,5},{5,4},{6,7},{7,6},{8,9},{9,8},{10,11... | collective-permute-start | bytes 1769480 | tf_op jit(solution)/shard_map/ppermute | solution.py:439
  71.5 6.3 %collective-permute-start.14 = (bf16[144,16,128]{2,1,0:T(8,128)(2,1)S(1)}, bf16[144,16,128]{2,1,0:T(8,128)(2,1)S(1)}, u32[]{:S(2)}, u32[]{:S(2)}) collective-permute-start(bf16[144,16,128]{2,1,0:T(8,128)(2,1)S(1)} %collective-permute-done.7.refs_3_), channel_id=1, source_target_pairs={{0,1},{1,0},{2,3},{3,2},{4,5},{5,4},{6,7},{7,6},{8,9},{9,8},{10,11... | collective-permute-start | bytes 1769480 | tf_op jit(solution)/shard_map/ppermute | solution.py:439
  73.8 5.7 %collective-permute-start.15 = (bf16[144,16,128]{2,1,0:T(8,128)(2,1)S(1)}, bf16[144,16,128]{2,1,0:T(8,128)(2,1)S(1)}, u32[]{:S(2)}, u32[]{:S(2)}) collective-permute-start(bf16[144,16,128]{2,1,0:T(8,128)(2,1)S(1)} %collective-permute-done.8.refs_4_), channel_id=1, source_target_pairs={{0,1},{1,0},{2,3},{3,2},{4,5},{5,4},{6,7},{7,6},{8,9},{9,8},{10,11... | collective-permute-start | bytes 1769480 | tf_op jit(solution)/shard_map/ppermute | solution.py:439
  77.9 2.5 %collective-permute-start.16 = (bf16[144,16,128]{2,1,0:T(8,128)(2,1)S(1)}, bf16[144,16,128]{2,1,0:T(8,128)(2,1)S(1)}, u32[]{:S(2)}, u32[]{:S(2)}) collective-permute-start(bf16[144,16,128]{2,1,0:T(8,128)(2,1)S(1)} %collective-permute-done.9.refs_5_), channel_id=1, source_target_pairs={{0,1},{1,0},{2,3},{3,2},{4,5},{5,4},{6,7},{7,6},{8,9},{9,8},{10,11... | collective-permute-start | bytes 1769480 | tf_op jit(solution)/shard_map/ppermute | solution.py:439
  80.3 2.0 %collective-permute-start.17 = (bf16[144,16,128]{2,1,0:T(8,128)(2,1)S(1)}, bf16[144,16,128]{2,1,0:T(8,128)(2,1)S(1)}, u32[]{:S(2)}, u32[]{:S(2)}) collective-permute-start(bf16[144,16,128]{2,1,0:T(8,128)(2,1)S(1)} %collective-permute-done.10.refs_6_), channel_id=1, source_target_pairs={{0,1},{1,0},{2,3},{3,2},{4,5},{5,4},{6,7},{7,6},{8,9},{9,8},{10,11... | collective-permute-start | bytes 1769480 | tf_op jit(solution)/shard_map/ppermute | solution.py:439
  80.7 2.5 %collective-permute-start.18 = (bf16[144,16,128]{2,1,0:T(8,128)(2,1)S(1)}, bf16[144,16,128]{2,1,0:T(8,128)(2,1)S(1)}, u32[]{:S(2)}, u32[]{:S(2)}) collective-permute-start(bf16[144,16,128]{2,1,0:T(8,128)(2,1)S(1)} %collective-permute-done.11.refs_7_), channel_id=1, source_target_pairs={{0,1},{1,0},{2,3},{3,2},{4,5},{5,4},{6,7},{7,6},{8,9},{9,8},{10,11... | collective-permute-start | bytes 1769480 | tf_op jit(solution)/shard_map/ppermute | solution.py:439
  83.2 16.9 %collective-permute-start.19 = (bf16[4608,128]{1,0:T(8,128)(2,1)S(1)}, bf16[4608,128]{1,0:T(8,128)(2,1)S(1)}, u32[]{:S(2)}, u32[]{:S(2)}) collective-permute-start(bf16[4608,128]{1,0:T(8,128)(2,1)S(1)} %shard_map.76.refs_4_), channel_id=1, source_target_pairs={{0,8},{1,3},{2,10},{3,5},{4,12},{5,7},{6,14},{7,1},{8,16},{9,11},{... | collective-permute-start | bytes 3538952 | tf_op jit(solution)/shard_map/ppermute | solution.py:439
  83.4 16.7 %collective-permute-start.20 = (bf16[4608,128]{1,0:T(8,128)(2,1)S(1)}, bf16[4608,128]{1,0:T(8,128)(2,1)S(1)}, u32[]{:S(2)}, u32[]{:S(2)}) collective-permute-start(bf16[4608,128]{1,0:T(8,128)(2,1)S(1)} %shard_map.76.refs_4_), channel_id=1, source_target_pairs={{0,24},{1,7},{2,26},{3,1},{4,28},{5,3},{6,30},{7,5},{8,0},{9,15},{... | collective-permute-start | bytes 3538952 | tf_op jit(solution)/shard_map/ppermute | solution.py:439
  100.1 19.8 %copy-start.1 = (f32[147456]{0:T(1024)S(1)}, f32[147456]{0:T(1024)}, u32[]{:S(2)}) copy-start(f32[147456]{0:T(1024)} %param.6) | copy-start | bytes 1769476
  100.1 19.7 %collective-permute-start.21 = (bf16[12288,128]{1,0:T(8,128)(2,1)S(1)}, bf16[12288,128]{1,0:T(8,128)(2,1)S(1)}, u32[]{:S(2)}, u32[]{:S(2)}) collective-permute-start(bf16[12288,128]{1,0:T(8,128)(2,1)S(1)} %shard_map.79.refs_0_), channel_id=1, source_target_pairs={{0,1},{1,0},{2,3},{3,2},{4,5},{5,4},{6,7},{7,6},{8,9},{9,8},{10,11... | collective-permute-start | bytes 9437192 | tf_op jit(solution)/shard_map/ppermute | solution.py:439
  102.1 16.6 %collective-permute-start.22 = (bf16[4608,128]{1,0:T(8,128)(2,1)S(1)}, bf16[4608,128]{1,0:T(8,128)(2,1)S(1)}, u32[]{:S(2)}, u32[]{:S(2)}) collective-permute-start(bf16[4608,128]{1,0:T(8,128)(2,1)S(1)} %collective-permute-done.19.refs_5_), channel_id=1, source_target_pairs={{0,8},{1,3},{2,10},{3,5},{4,12},{5,7},{6,14},{7,1},{8,16},{9,11},{... | collective-permute-start | bytes 3538952 | tf_op jit(solution)/shard_map/ppermute | solution.py:439
  102.3 17.5 %collective-permute-start.24 = (bf16[4608,128]{1,0:T(8,128)(2,1)S(1)}, bf16[4608,128]{1,0:T(8,128)(2,1)S(1)}, u32[]{:S(2)}, u32[]{:S(2)}) collective-permute-start(bf16[4608,128]{1,0:T(8,128)(2,1)S(1)} %collective-permute-done.19.refs_5_), channel_id=1, source_target_pairs={{0,1},{1,0},{2,3},{3,2},{4,5},{5,4},{6,7},{7,6},{8,9},{9,8},{10,11... | collective-permute-start | bytes 3538952 | tf_op jit(solution)/shard_map/ppermute | solution.py:439
  102.5 17.3 %collective-permute-start.23 = (bf16[4608,128]{1,0:T(8,128)(2,1)S(1)}, bf16[4608,128]{1,0:T(8,128)(2,1)S(1)}, u32[]{:S(2)}, u32[]{:S(2)}) collective-permute-start(bf16[4608,128]{1,0:T(8,128)(2,1)S(1)} %shard_map.76.refs_4_), channel_id=1, source_target_pairs={{0,1},{1,0},{2,3},{3,2},{4,5},{5,4},{6,7},{7,6},{8,9},{9,8},{10,11... | collective-permute-start | bytes 3538952 | tf_op jit(solution)/shard_map/ppermute | solution.py:439
  102.8 17.0 %collective-permute-start.25 = (bf16[4608,128]{1,0:T(8,128)(2,1)S(1)}, bf16[4608,128]{1,0:T(8,128)(2,1)S(1)}, u32[]{:S(2)}, u32[]{:S(2)}) collective-permute-start(bf16[4608,128]{1,0:T(8,128)(2,1)S(1)} %collective-permute-done.20.refs_6_), channel_id=1, source_target_pairs={{0,1},{1,0},{2,3},{3,2},{4,5},{5,4},{6,7},{7,6},{8,9},{9,8},{10,11... | collective-permute-start | bytes 3538952 | tf_op jit(solution)/shard_map/ppermute | solution.py:439
  118.7 7.5 %collective-permute-start.26 = (bf16[4608,128]{1,0:T(8,128)(2,1)S(1)}, bf16[4608,128]{1,0:T(8,128)(2,1)S(1)}, u32[]{:S(2)}, u32[]{:S(2)}) collective-permute-start(bf16[4608,128]{1,0:T(8,128)(2,1)S(1)} %collective-permute-done.22.refs_7_), channel_id=1, source_target_pairs={{0,1},{1,0},{2,3},{3,2},{4,5},{5,4},{6,7},{7,6},{8,9},{9,8},{10,11... | collective-permute-start | bytes 3538952 | tf_op jit(solution)/shard_map/ppermute | solution.py:439
  (2 other events, 11.1 us)
where the time goes:
time: 128 us
  starting transfers between devices  50.2 us (39%)
  Pallas kernels  41.4 us (32%)
  waiting for transfers between devices  33.6 us (26%)
  local copies, waits for them, and re-layouts  1.66 us (1%)
    ppermute x27, starting transfers between devices, send(): return lax.ppermute(block, 'shard', route)  35.8 us
    pallas_call x2, Pallas kernels, orthogonalized(): pl.pallas_call(lambda *refs: matrix_kernel(last, *refs), out_shape=jax.Sh...  29.3 us
    ppermute x27, waiting for transfers between devices, send(): return lax.ppermute(block, 'shard', route)  20.4 us
    all_to_all x1, starting transfers between devices, on_device(): sums = lax.all_to_all(sums, 'group', 0, 0)  8.19 us
    all_to_all x1, waiting for transfers between devices, on_device(): sums = lax.all_to_all(sums, 'shard', 0, 0)  6.79 us
    all_to_all x1, waiting for transfers between devices, on_device(): sums = lax.all_to_all(sums, 'group', 0, 0)  6.37 us
    pallas_call x1, Pallas kernels, on_device(): pl.pallas_call(finish_kernel, out_shape=(weights_shape, flat_shape, flat_...  6.3 us
    all_to_all x1, starting transfers between devices, on_device(): sums = lax.all_to_all(sums, 'shard', 0, 0)  6.25 us
  transfers between devices with their start and end apart: 29, of which 11 were waited for; matrix products, arithmetic and copies ran while one was open for 0% of the time, Pallas kernels for 28%

commit v1 on v0

--- a/solution.py
+++ b/solution.py
@@ -216,9 +216,9 @@
         top = jnp.where(same, step[:WIDE], 0.0)
         diagonal_row.append(jnp.sum(top, axis=0, keepdims=True))
         diagonal_column.append(jnp.sum(top, axis=1, keepdims=True))
-        rest[part, part] = jnp.where(same, 0.0, step[:WIDE]).astype(bf16)
+        rest[part, part] = (jnp.where(same, 0.0, step[:WIDE]) * scale).astype(bf16)
         if n < 2:
-            rest[lower[n + 1], part] = step[WIDE:].astype(bf16)
+            rest[lower[n + 1], part] = (step[WIDE:] * scale).astype(bf16)
         mirror(rest, n)
     diagonal_column = jnp.concatenate(diagonal_column, 0)
     diagonal_row = (jnp.concatenate(diagonal_row, 1) + coef_first * coef_first) * scale
@@ -228,7 +228,7 @@
     def _():
         def chunk(i, carry):
             block = jnp.concatenate([tiles(x, base + 192 * i + j, 32, 6) for j in range(6)], 1)
-            moved = mm(block, rest[...]) * scale + block.astype(f32) * diagonal_row
+            moved = mm(block, rest[...]) + block.astype(f32) * diagonal_row
             for j in range(6):
                 rows = pl.ds(3072 * i + j, 2 * WIDE, stride=6)
                 flat[rows, :] = moved[:, 128 * j : 128 * j + 128]
@@ -242,7 +242,7 @@
     def _():
         def chunk(i, carry):
             block = wide[:, pl.ds(pl.multiple_of(WIDE * i, WIDE), WIDE)]
-            moved = mm(rest[...], block) * scale + block.astype(f32) * diagonal_column
+            moved = mm(rest[...], block) + block.astype(f32) * diagonal_column
             for h in range(2):
                 panel = moved[:, 128 * h : 128 * h + 128]
                 start = 2 * i + h
@@ -288,7 +288,7 @@
 
 def matrix_kernel(last, *refs):
     info, sources, refs = refs[0], refs[1:15], refs[15:]
-    result, x, wide, flat, a0, b0, wb, b1, total, out_block, sems, more = refs
+    result, x, wide, flat, a0, b0, wb, b1, total, sems = refs
     group, shard = info[24], info[25]
     matrix = jnp.int32(2) if last else shard % 2
     first = (UNITS * matrix) // 3
@@ -311,18 +311,11 @@
     kind = kind_of(info, 3 * group + matrix)
     base = MAT_TILES * matrix - SHARD_TILES * first
 
-    def store(i):
-        rows = pl.ds(pl.multiple_of(1536 * i, 1536), 1536)
-        return pltpu.make_async_copy(out_block.at[rows, :], result.at[rows, :], more.at[i])
-
     def emit(i):
         rows = pl.ds(pl.multiple_of(1536 * i, 1536), 1536)
-        out_block[rows, :] = flat[rows, :].astype(bf16)
-        store(i).start()
+        result[rows, :] = flat[rows, :].astype(bf16)
 
     orthogonalize(kind, base, x, wide, flat, a0, b0, wb, b1, total, emit)
-    for i in range(8):
-        store(i).wait()
 
 
 HOPS = (0, 1, 3, 2)
@@ -345,9 +338,7 @@
     pltpu.VMEM((FF, FF), bf16),
     pltpu.VMEM((FF, FF), bf16),
     pltpu.VMEM((FF, FF), f32),
-    pltpu.VMEM((MAT_ROWS, 128), bf16),
     pltpu.SemaphoreType.DMA((32,)),
-    pltpu.SemaphoreType.DMA((8,)),
 ]
 
 
@@ -478,9 +469,8 @@
     early = [whole, forward[0], backward[1], forward[1], backward[0]]
     swapped = [send(block, swap_route()) for block in early]
     across, swapped = lax.optimization_barrier((across, swapped))
+    quad, across = lax.optimization_barrier((quad, across))
     sources = early + across + swapped + [send(block, swap_route()) for block in across]
-
-    quad, sources = lax.optimization_barrier((quad, sources))
     masters = [quad, send(quad, second_route(1)), send(quad, second_route(3))]
 
     cost = pl.CostEstimate(flops=9_300_000_000, bytes_accessed=20_000_000, transcendentals=0)
@@ -490,7 +480,7 @@
             lambda *refs: matrix_kernel(last, *refs),
             out_shape=jax.ShapeDtypeStruct((MAT_ROWS, 128), bf16),
             in_specs=[SM] + [HBM] * 14,
-            out_specs=VM if last else ANY,
+            out_specs=VM,
             scratch_shapes=MATRIX_SCRATCH,
             compiler_params=params(29),
             cost_estimate=cost,

time: 128 us -> 124 us (0.969)
  Pallas kernels: 41.4 us -> 37.1 us
    pallas_call x2, Pallas kernels: 29.3 us -> 25.1 us  [orthogonalized(): pl.pallas_call(lambda *refs: matrix_kernel(last, *refs), out_shape=jax.Sh...]
  transfers between devices with their start and end apart: 29 -> 29, of which waited for: 11 -> 10; matrix products, arithmetic and copies ran while one was open for 0% -> 0% of each run, Pallas kernels for 28% -> 25%
where the time goes in v1:
time: 124 us
  starting transfers between devices  49.5 us (40%)
  Pallas kernels  37.1 us (30%)
  waiting for transfers between devices  34.8 us (28%)
  local copies, waits for them, and re-layouts  1.66 us (1%)
    ppermute x27, starting transfers between devices, send(): return lax.ppermute(block, 'shard', route)  35 us
    pallas_call x2, Pallas kernels, orthogonalized(): pl.pallas_call(lambda *refs: matrix_kernel(last, *refs), out_shape=jax.Sh...  25.1 us
    ppermute x27, waiting for transfers between devices, send(): return lax.ppermute(block, 'shard', route)  21.6 us
    all_to_all x1, starting transfers between devices, on_device(): sums = lax.all_to_all(sums, 'group', 0, 0)  8.19 us
    all_to_all x1, waiting for transfers between devices, on_device(): sums = lax.all_to_all(sums, 'shard', 0, 0)  6.79 us
    all_to_all x1, waiting for transfers between devices, on_device(): sums = lax.all_to_all(sums, 'group', 0, 0)  6.37 us
    pallas_call x1, Pallas kernels, on_device(): pl.pallas_call(finish_kernel, out_shape=(weights_shape, flat_shape, flat_...  6.3 us
    all_to_all x1, starting transfers between devices, on_device(): sums = lax.all_to_all(sums, 'shard', 0, 0)  6.25 us
  transfers between devices with their start and end apart: 29, of which 10 were waited for; matrix products, arithmetic and copies ran while one was open for 0% of the time, Pallas kernels for 25%

profile of v1, /device:TPU:1, one launch (start us, length us, event | category | flops | bytes accessed | tf_op | source)
XLA Modules:
  0.0 124.2 jit_solution(6132403141538881534)
XLA Ops:
  0.6 2.0 %shard_map.75 = (f32[32,128]{1,0:T(8,128)}, bf16[1152,128]{1,0:T(8,128)(2,1)}) custom-call(f32[1152,128]{1,0:T(8,128)} %bitcast.14, f32[1152,128]{1,0:T(8,128)} %bitcast.16), custom_call_target="tpu_custom_call" | custom-call | tf_op jit(solution)/shard_map/pallas_call | solution.py:432
  2.6 2.1 %collective-permute-start = (bf16[1152,128]{1,0:T(8,128)(2,1)}, bf16[1152,128]{1,0:T(8,128)(2,1)S(1)}, u32[]{:S(2)}, u32[]{:S(2)}) collective-permute-start(bf16[1152,128]{1,0:T(8,128)(2,1)} %get-tuple-element.35.refs_0_), channel_id=1, source_target_pairs={{0,2},{1,9},{2,4},{3,11},{4,6},{5,13},{6,0},{7,15},{8,10},{9,17},{... | collective-permute-start | bytes 884744 | tf_op jit(solution)/shard_map/ppermute | solution.py:430
  4.8 2.5 %collective-permute-start.1 = (bf16[1152,128]{1,0:T(8,128)(2,1)}, bf16[1152,128]{1,0:T(8,128)(2,1)S(1)}, u32[]{:S(2)}, u32[]{:S(2)}) collective-permute-start(bf16[1152,128]{1,0:T(8,128)(2,1)} %get-tuple-element.35.refs_0_), channel_id=1, source_target_pairs={{0,4},{1,17},{2,6},{3,19},{4,0},{5,21},{6,2},{7,23},{8,12},{9,25},... | collective-permute-start | bytes 884744 | tf_op jit(solution)/shard_map/ppermute | solution.py:430
  7.2 1.2 collective-permute-start.2
  8.4 6.3 %all-to-all-start = ((f32[32,1,128]{2,1,0:T(1,128)}), f32[32,1,128]{2,1,0:T(1,128)S(1)}, u32[]{:S(2)}, u32[]{:S(2)}) async-start(f32[32,1,128]{2,1,0:T(1,128)} %bitcast.21), calls=%async_computation | async-start | bytes 32768 | tf_op jit(solution)/shard_map/all_to_all | solution.py:448
  14.7 6.8 %all-to-all-done = f32[32,1,128]{2,1,0:T(1,128)S(1)} async-done(((f32[32,1,128]{2,1,0:T(1,128)}), f32[32,1,128]{2,1,0:T(1,128)S(1)}, u32[]{:S(2)}, u32[]{:S(2)}) %all-to-all-start) | async-done | bytes 16416 | tf_op jit(solution)/shard_map/all_to_all | solution.py:448
  21.6 1.0 copy-done.3
  23.3 8.2 %all-to-all-start.1 = ((f32[8,1,128]{2,1,0:T(1,128)}), f32[8,1,128]{2,1,0:T(1,128)S(1)}, u32[]{:S(2)}, u32[]{:S(2)}) async-start(f32[8,1,128]{2,1,0:T(1,128)} %bitcast.6), calls=%async_computation.1 | async-start | bytes 8192 | tf_op jit(solution)/shard_map/all_to_all | solution.py:452
  31.6 6.4 %all-to-all-done.1 = f32[8,1,128]{2,1,0:T(1,128)S(1)} async-done(((f32[8,1,128]{2,1,0:T(1,128)}), f32[8,1,128]{2,1,0:T(1,128)S(1)}, u32[]{:S(2)}, u32[]{:S(2)}) %all-to-all-start.1) | async-done | bytes 4128 | tf_op jit(solution)/shard_map/all_to_all | solution.py:452
  38.0 1.7 %shard_map.77 = (f32[1152,128]{1,0:T(8,128)}, bf16[72,16,128]{2,1,0:T(8,128)(2,1)S(1)}) custom-call(s32[58]{0:T(128)S(1)} %pad_add_fusion.info.refs_0_, f32[8,128]{1,0:T(8,128)S(1)} %bitcast.19, f32[1152,128]{1,0:T(8,128)S(1)} %bitcast.15, f32[1152,128]{1,0:T(8,128)S(1)} %bitcast.18), custom_call_target="tpu_custom_call" | custom-call | tf_op jit(solution)/shard_map/pallas_call | solution.py:455
  40.0 1.7 %collective-permute-start.4 = (bf16[72,16,128]{2,1,0:T(8,128)(2,1)S(1)}, bf16[72,16,128]{2,1,0:T(8,128)(2,1)S(1)}, u32[]{:S(2)}, u32[]{:S(2)}) collective-permute-start(bf16[72,16,128]{2,1,0:T(8,128)(2,1)S(1)} %get-tuple-element.39.refs_0_), channel_id=1, source_target_pairs={{0,4},{1,17},{2,6},{3,19},{4,0},{5,21},{6,2},{7,23},{8,12},{9,25},... | collective-permute-start | bytes 884744 | tf_op jit(solution)/shard_map/ppermute | solution.py:430
  41.7 1.0 collective-permute-start.5
  42.7 7.2 %collective-permute-done.3.refs_1_ = bf16[72,16,128]{2,1,0:T(8,128)(2,1)S(1)} collective-permute-done((bf16[72,16,128]{2,1,0:T(8,128)(2,1)S(1)}, bf16[72,16,128]{2,1,0:T(8,128)(2,1)S(1)}, u32[]{:S(2)}, u32[]{:S(2)}) %collective-permute-start.3) | collective-permute-done | bytes 294944 | tf_op jit(solution)/shard_map/ppermute | solution.py:430
  51.1 2.4 %collective-permute-start.7 = (bf16[144,16,128]{2,1,0:T(8,128)(2,1)S(1)}, bf16[144,16,128]{2,1,0:T(8,128)(2,1)S(1)}, u32[]{:S(2)}, u32[]{:S(2)}) collective-permute-start(bf16[144,16,128]{2,1,0:T(8,128)(2,1)S(1)} %get-tuple-element.44), channel_id=1, source_target_pairs={{0,24},{1,7},{2,26},{3,1},{4,28},{5,3},{6,30},{7,5},{8,0},{9,15},{... | collective-permute-start | bytes 1769480 | tf_op jit(solution)/shard_map/ppermute | solution.py:430
  53.5 2.7 %collective-permute-start.9 = (bf16[144,16,128]{2,1,0:T(8,128)(2,1)S(1)}, bf16[144,16,128]{2,1,0:T(8,128)(2,1)S(1)}, u32[]{:S(2)}, u32[]{:S(2)}) collective-permute-start(bf16[144,16,128]{2,1,0:T(8,128)(2,1)S(1)} %get-tuple-element.41), channel_id=1, source_target_pairs={{0,24},{1,7},{2,26},{3,1},{4,28},{5,3},{6,30},{7,5},{8,0},{9,15},{... | collective-permute-start | bytes 1769480 | tf_op jit(solution)/shard_map/ppermute | solution.py:430
  56.1 4.9 %collective-permute-done.6.refs_2_ = bf16[144,16,128]{2,1,0:T(8,128)(2,1)S(1)} collective-permute-done((bf16[144,16,128]{2,1,0:T(8,128)(2,1)S(1)}, bf16[144,16,128]{2,1,0:T(8,128)(2,1)S(1)}, u32[]{:S(2)}, u32[]{:S(2)}) %collective-permute-start.6) | collective-permute-done | bytes 589856 | tf_op jit(solution)/shard_map/ppermute | solution.py:430
  61.0 2.7 %collective-permute-start.11 = (bf16[144,16,128]{2,1,0:T(8,128)(2,1)S(1)}, bf16[144,16,128]{2,1,0:T(8,128)(2,1)S(1)}, u32[]{:S(2)}, u32[]{:S(2)}) collective-permute-start(bf16[144,16,128]{2,1,0:T(8,128)(2,1)S(1)} %collective-permute-done.7.refs_3_), channel_id=1, source_target_pairs={{0,24},{1,7},{2,26},{3,1},{4,28},{5,3},{6,30},{7,5},{8,0},{9,15},{... | collective-permute-start | bytes 1769480 | tf_op jit(solution)/shard_map/ppermute | solution.py:430
  63.7 4.6 %collective-permute-start.12 = (bf16[288,16,128]{2,1,0:T(8,128)(2,1)S(1)}, bf16[288,16,128]{2,1,0:T(8,128)(2,1)S(1)}, u32[]{:S(2)}, u32[]{:S(2)}) collective-permute-start(bf16[288,16,128]{2,1,0:T(8,128)(2,1)S(1)} %get-tuple-element.42.refs_1_), channel_id=1, source_target_pairs={{0,1},{1,0},{2,3},{3,2},{4,5},{5,4},{6,7},{7,6},{8,9},{9,8},{10,11... | collective-permute-start | bytes 3538952 | tf_op jit(solution)/shard_map/ppermute | solution.py:430
  68.3 3.1 %collective-permute-start.13 = (bf16[144,16,128]{2,1,0:T(8,128)(2,1)S(1)}, bf16[144,16,128]{2,1,0:T(8,128)(2,1)S(1)}, u32[]{:S(2)}, u32[]{:S(2)}) collective-permute-start(bf16[144,16,128]{2,1,0:T(8,128)(2,1)S(1)} %collective-permute-done.6.refs_2_), channel_id=1, source_target_pairs={{0,1},{1,0},{2,3},{3,2},{4,5},{5,4},{6,7},{7,6},{8,9},{9,8},{10,11... | collective-permute-start | bytes 1769480 | tf_op jit(solution)/shard_map/ppermute | solution.py:430
  71.4 2.2 %collective-permute-done.10.refs_6_ = bf16[144,16,128]{2,1,0:T(8,128)(2,1)S(1)} collective-permute-done((bf16[144,16,128]{2,1,0:T(8,128)(2,1)S(1)}, bf16[144,16,128]{2,1,0:T(8,128)(2,1)S(1)}, u32[]{:S(2)}, u32[]{:S(2)}) %collective-permute-start.10) | collective-permute-done | bytes 589856 | tf_op jit(solution)/shard_map/ppermute | solution.py:430
  73.7 4.1 %collective-permute-start.15 = (bf16[144,16,128]{2,1,0:T(8,128)(2,1)S(1)}, bf16[144,16,128]{2,1,0:T(8,128)(2,1)S(1)}, u32[]{:S(2)}, u32[]{:S(2)}) collective-permute-start(bf16[144,16,128]{2,1,0:T(8,128)(2,1)S(1)} %collective-permute-done.8.refs_4_), channel_id=1, source_target_pairs={{0,1},{1,0},{2,3},{3,2},{4,5},{5,4},{6,7},{7,6},{8,9},{9,8},{10,11... | collective-permute-start | bytes 1769480 | tf_op jit(solution)/shard_map/ppermute | solution.py:430
  77.8 1.6 %collective-permute-done.15.refs_11_ = bf16[144,16,128]{2,1,0:T(8,128)(2,1)S(1)} collective-permute-done((bf16[144,16,128]{2,1,0:T(8,128)(2,1)S(1)}, bf16[144,16,128]{2,1,0:T(8,128)(2,1)S(1)}, u32[]{:S(2)}, u32[]{:S(2)}) %collective-permute-start.15) | collective-permute-done | bytes 589856 | tf_op jit(solution)/shard_map/ppermute | solution.py:430
  79.4 0.8 collective-permute-done.16.refs_12_
  80.9 2.4 %collective-permute-start.20 = (bf16[4608,128]{1,0:T(8,128)(2,1)S(1)}, bf16[4608,128]{1,0:T(8,128)(2,1)S(1)}, u32[]{:S(2)}, u32[]{:S(2)}) collective-permute-start(bf16[4608,128]{1,0:T(8,128)(2,1)S(1)} %shard_map.76.refs_4_), channel_id=1, source_target_pairs={{0,24},{1,7},{2,26},{3,1},{4,28},{5,3},{6,30},{7,5},{8,0},{9,15},{... | collective-permute-start | bytes 3538952 | tf_op jit(solution)/shard_map/ppermute | solution.py:430
  83.4 12.6 %shard_map.79.refs_0_ = bf16[12288,128]{1,0:T(8,128)(2,1)S(1)} custom-call(s32[58]{0:T(128)S(1)} %pad_add_fusion.info.refs_0_, bf16[288,16,128]{2,1,0:T(8,128)(2,1)S(1)} %get-tuple-element.42.refs_1_, bf16[144,16,128]{2,1,0:T(8,128)(2,1)S(1)} %collective-permute-done.6.refs_2_, bf16[144,16,128]{2,1,0:T(8,128)(2,1)S(1)} %collective-permute-done.7.refs_3_, ...), custom_call_target="tpu_custom_call" | custom-call | flops 9299999744 | bytes 20000000 | tf_op jit(solution)/shard_map/pallas_call | solution.py:479
  96.0 1.2 collective-permute-done.19.refs_5_
  97.3 1.2 collective-permute-start.21
  99.6 12.5 %shard_map.80.refs_2_ = bf16[12288,128]{1,0:T(8,128)(2,1)S(1)} custom-call(s32[58]{0:T(128)S(1)} %pad_add_fusion.info.refs_0_, bf16[288,16,128]{2,1,0:T(8,128)(2,1)S(1)} %get-tuple-element.42.refs_1_, bf16[144,16,128]{2,1,0:T(8,128)(2,1)S(1)} %collective-permute-done.6.refs_2_, bf16[144,16,128]{2,1,0:T(8,128)(2,1)S(1)} %collective-permute-done.7.refs_3_, ...), custom_call_target="tpu_custom_call" | custom-call | flops 9299999744 | bytes 20000000 | tf_op jit(solution)/shard_map/pallas_call | solution.py:479
  112.1 2.9 %collective-permute-done.22.refs_7_ = bf16[4608,128]{1,0:T(8,128)(2,1)S(1)} collective-permute-done((bf16[4608,128]{1,0:T(8,128)(2,1)S(1)}, bf16[4608,128]{1,0:T(8,128)(2,1)S(1)}, u32[]{:S(2)}, u32[]{:S(2)}) %collective-permute-start.22) | collective-permute-done | bytes 1179680 | tf_op jit(solution)/shard_map/ppermute | solution.py:430
  115.1 0.9 collective-permute-start.26
  116.0 6.3 %shard_map.81 = (bf16[36864,128]{1,0:T(8,128)(2,1)}, f32[1152,128]{1,0:T(8,128)}, f32[1152,128]{1,0:T(8,128)}, bf16[4608,128]{1,0:T(8,128)(2,1)S(1)}) custom-call(s32[58]{0:T(128)S(1)} %pad_add_fusion.info.refs_0_, bf16[12288,128]{1,0:T(8,128)(2,1)S(1)} %shard_map.79.refs_0_, bf16[12288,128]{1,0:T(8,128)(2,1)S(1)} %collective-permute-done.21.refs_1_, ...), custom_call_target="tpu_custom_call" | custom-call | flops 10000000 | bytes 28000000 | tf_op jit(solution)/shard_map/pallas_call | solution.py:499
  122.3 1.7 %shard_map.82 = bf16[36864,128]{1,0:T(8,128)(2,1)} custom-call(s32[58]{0:T(128)S(1)} %pad_add_fusion.info.refs_0_, bf16[36864,128]{1,0:T(8,128)(2,1)} %get-tuple-element.63._, bf16[4608,128]{1,0:T(8,128)(2,1)S(1)} %get-tuple-element.64.rest, bf16[4608,128]{1,0:T(8,128)(2,1)S(1)} %collective-permute-done.26.masters), custom_call_target="tpu_custom_call", output_to_operand_aliasing={{}: (1, {})} | custom-call | tf_op jit(solution)/shard_map/pallas_call | solution.py:513
  (48 shorter events, 4.2 us)
Async XLA Ops:
  2.6 18.9 %collective-permute-start = (bf16[1152,128]{1,0:T(8,128)(2,1)}, bf16[1152,128]{1,0:T(8,128)(2,1)S(1)}, u32[]{:S(2)}, u32[]{:S(2)}) collective-permute-start(bf16[1152,128]{1,0:T(8,128)(2,1)} %get-tuple-element.35.refs_0_), channel_id=1, source_target_pairs={{0,2},{1,9},{2,4},{3,11},{4,6},{5,13},{6,0},{7,15},{8,10},{9,17},{... | collective-permute-start | bytes 884744 | tf_op jit(solution)/shard_map/ppermute | solution.py:430
  4.8 16.8 %collective-permute-start.1 = (bf16[1152,128]{1,0:T(8,128)(2,1)}, bf16[1152,128]{1,0:T(8,128)(2,1)S(1)}, u32[]{:S(2)}, u32[]{:S(2)}) collective-permute-start(bf16[1152,128]{1,0:T(8,128)(2,1)} %get-tuple-element.35.refs_0_), channel_id=1, source_target_pairs={{0,4},{1,17},{2,6},{3,19},{4,0},{5,21},{6,2},{7,23},{8,12},{9,25},... | collective-permute-start | bytes 884744 | tf_op jit(solution)/shard_map/ppermute | solution.py:430
  7.2 14.4 %collective-permute-start.2 = (bf16[1152,128]{1,0:T(8,128)(2,1)}, bf16[1152,128]{1,0:T(8,128)(2,1)S(1)}, u32[]{:S(2)}, u32[]{:S(2)}) collective-permute-start(bf16[1152,128]{1,0:T(8,128)(2,1)} %get-tuple-element.35.refs_0_), channel_id=1, source_target_pairs={{0,6},{1,25},{2,0},{3,27},{4,2},{5,29},{6,4},{7,31},{8,14},{9,1},{... | collective-permute-start | bytes 884744 | tf_op jit(solution)/shard_map/ppermute | solution.py:430
  8.4 13.1 %all-to-all-start = ((f32[32,1,128]{2,1,0:T(1,128)}), f32[32,1,128]{2,1,0:T(1,128)S(1)}, u32[]{:S(2)}, u32[]{:S(2)}) async-start(f32[32,1,128]{2,1,0:T(1,128)} %bitcast.21), calls=%async_computation | async-start | bytes 32768 | tf_op jit(solution)/shard_map/all_to_all | solution.py:448
  21.5 16.4 %copy-start = (f32[147456]{0:T(1024)S(1)}, f32[147456]{0:T(1024)}, u32[]{:S(2)}) copy-start(f32[147456]{0:T(1024)} %param.4) | copy-start | bytes 1769476
  21.5 16.4 %copy-start.2 = (f32[147456]{0:T(1024)S(1)}, f32[147456]{0:T(1024)}, u32[]{:S(2)}) copy-start(f32[147456]{0:T(1024)} %param.5) | copy-start | bytes 1769476
  23.3 14.6 %all-to-all-start.1 = ((f32[8,1,128]{2,1,0:T(1,128)}), f32[8,1,128]{2,1,0:T(1,128)S(1)}, u32[]{:S(2)}, u32[]{:S(2)}) async-start(f32[8,1,128]{2,1,0:T(1,128)} %bitcast.6), calls=%async_computation.1 | async-start | bytes 8192 | tf_op jit(solution)/shard_map/all_to_all | solution.py:452
  39.7 10.2 %collective-permute-start.3 = (bf16[72,16,128]{2,1,0:T(8,128)(2,1)S(1)}, bf16[72,16,128]{2,1,0:T(8,128)(2,1)S(1)}, u32[]{:S(2)}, u32[]{:S(2)}) collective-permute-start(bf16[72,16,128]{2,1,0:T(8,128)(2,1)S(1)} %get-tuple-element.39.refs_0_), channel_id=1, source_target_pairs={{0,2},{1,9},{2,4},{3,11},{4,6},{5,13},{6,0},{7,15},{8,10},{9,17},{... | collective-permute-start | bytes 884744 | tf_op jit(solution)/shard_map/ppermute | solution.py:430
  40.0 9.9 %collective-permute-start.4 = (bf16[72,16,128]{2,1,0:T(8,128)(2,1)S(1)}, bf16[72,16,128]{2,1,0:T(8,128)(2,1)S(1)}, u32[]{:S(2)}, u32[]{:S(2)}) collective-permute-start(bf16[72,16,128]{2,1,0:T(8,128)(2,1)S(1)} %get-tuple-element.39.refs_0_), channel_id=1, source_target_pairs={{0,4},{1,17},{2,6},{3,19},{4,0},{5,21},{6,2},{7,23},{8,12},{9,25},... | collective-permute-start | bytes 884744 | tf_op jit(solution)/shard_map/ppermute | solution.py:430
  41.7 8.8 %collective-permute-start.5 = (bf16[72,16,128]{2,1,0:T(8,128)(2,1)S(1)}, bf16[72,16,128]{2,1,0:T(8,128)(2,1)S(1)}, u32[]{:S(2)}, u32[]{:S(2)}) collective-permute-start(bf16[72,16,128]{2,1,0:T(8,128)(2,1)S(1)} %get-tuple-element.39.refs_0_), channel_id=1, source_target_pairs={{0,6},{1,25},{2,0},{3,27},{4,2},{5,29},{6,4},{7,31},{8,14},{9,1},{... | collective-permute-start | bytes 884744 | tf_op jit(solution)/shard_map/ppermute | solution.py:430
  50.7 10.3 %collective-permute-start.6 = (bf16[144,16,128]{2,1,0:T(8,128)(2,1)S(1)}, bf16[144,16,128]{2,1,0:T(8,128)(2,1)S(1)}, u32[]{:S(2)}, u32[]{:S(2)}) collective-permute-start(bf16[144,16,128]{2,1,0:T(8,128)(2,1)S(1)} %get-tuple-element.41), channel_id=1, source_target_pairs={{0,8},{1,3},{2,10},{3,5},{4,12},{5,7},{6,14},{7,1},{8,16},{9,11},{... | collective-permute-start | bytes 1769480 | tf_op jit(solution)/shard_map/ppermute | solution.py:430
  51.1 10.0 %collective-permute-start.7 = (bf16[144,16,128]{2,1,0:T(8,128)(2,1)S(1)}, bf16[144,16,128]{2,1,0:T(8,128)(2,1)S(1)}, u32[]{:S(2)}, u32[]{:S(2)}) collective-permute-start(bf16[144,16,128]{2,1,0:T(8,128)(2,1)S(1)} %get-tuple-element.44), channel_id=1, source_target_pairs={{0,24},{1,7},{2,26},{3,1},{4,28},{5,3},{6,30},{7,5},{8,0},{9,15},{... | collective-permute-start | bytes 1769480 | tf_op jit(solution)/shard_map/ppermute | solution.py:430
  53.4 14.9 %collective-permute-start.8 = (bf16[144,16,128]{2,1,0:T(8,128)(2,1)S(1)}, bf16[144,16,128]{2,1,0:T(8,128)(2,1)S(1)}, u32[]{:S(2)}, u32[]{:S(2)}) collective-permute-start(bf16[144,16,128]{2,1,0:T(8,128)(2,1)S(1)} %get-tuple-element.44), channel_id=1, source_target_pairs={{0,8},{1,3},{2,10},{3,5},{4,12},{5,7},{6,14},{7,1},{8,16},{9,11},{... | collective-permute-start | bytes 1769480 | tf_op jit(solution)/shard_map/ppermute | solution.py:430
  53.5 18.0 %collective-permute-start.9 = (bf16[144,16,128]{2,1,0:T(8,128)(2,1)S(1)}, bf16[144,16,128]{2,1,0:T(8,128)(2,1)S(1)}, u32[]{:S(2)}, u32[]{:S(2)}) collective-permute-start(bf16[144,16,128]{2,1,0:T(8,128)(2,1)S(1)} %get-tuple-element.41), channel_id=1, source_target_pairs={{0,24},{1,7},{2,26},{3,1},{4,28},{5,3},{6,30},{7,5},{8,0},{9,15},{... | collective-permute-start | bytes 1769480 | tf_op jit(solution)/shard_map/ppermute | solution.py:430
  61.0 12.6 %collective-permute-start.10 = (bf16[144,16,128]{2,1,0:T(8,128)(2,1)S(1)}, bf16[144,16,128]{2,1,0:T(8,128)(2,1)S(1)}, u32[]{:S(2)}, u32[]{:S(2)}) collective-permute-start(bf16[144,16,128]{2,1,0:T(8,128)(2,1)S(1)} %collective-permute-done.6.refs_2_), channel_id=1, source_target_pairs={{0,8},{1,3},{2,10},{3,5},{4,12},{5,7},{6,14},{7,1},{8,16},{9,11},{... | collective-permute-start | bytes 1769480 | tf_op jit(solution)/shard_map/ppermute | solution.py:430
  61.0 16.7 %collective-permute-start.11 = (bf16[144,16,128]{2,1,0:T(8,128)(2,1)S(1)}, bf16[144,16,128]{2,1,0:T(8,128)(2,1)S(1)}, u32[]{:S(2)}, u32[]{:S(2)}) collective-permute-start(bf16[144,16,128]{2,1,0:T(8,128)(2,1)S(1)} %collective-permute-done.7.refs_3_), channel_id=1, source_target_pairs={{0,24},{1,7},{2,26},{3,1},{4,28},{5,3},{6,30},{7,5},{8,0},{9,15},{... | collective-permute-start | bytes 1769480 | tf_op jit(solution)/shard_map/ppermute | solution.py:430
  63.7 16.5 %collective-permute-start.12 = (bf16[288,16,128]{2,1,0:T(8,128)(2,1)S(1)}, bf16[288,16,128]{2,1,0:T(8,128)(2,1)S(1)}, u32[]{:S(2)}, u32[]{:S(2)}) collective-permute-start(bf16[288,16,128]{2,1,0:T(8,128)(2,1)S(1)} %get-tuple-element.42.refs_1_), channel_id=1, source_target_pairs={{0,1},{1,0},{2,3},{3,2},{4,5},{5,4},{6,7},{7,6},{8,9},{9,8},{10,11... | collective-permute-start | bytes 3538952 | tf_op jit(solution)/shard_map/ppermute | solution.py:430
  68.3 9.4 %collective-permute-start.13 = (bf16[144,16,128]{2,1,0:T(8,128)(2,1)S(1)}, bf16[144,16,128]{2,1,0:T(8,128)(2,1)S(1)}, u32[]{:S(2)}, u32[]{:S(2)}) collective-permute-start(bf16[144,16,128]{2,1,0:T(8,128)(2,1)S(1)} %collective-permute-done.6.refs_2_), channel_id=1, source_target_pairs={{0,1},{1,0},{2,3},{3,2},{4,5},{5,4},{6,7},{7,6},{8,9},{9,8},{10,11... | collective-permute-start | bytes 1769480 | tf_op jit(solution)/shard_map/ppermute | solution.py:430
  71.4 6.3 %collective-permute-start.14 = (bf16[144,16,128]{2,1,0:T(8,128)(2,1)S(1)}, bf16[144,16,128]{2,1,0:T(8,128)(2,1)S(1)}, u32[]{:S(2)}, u32[]{:S(2)}) collective-permute-start(bf16[144,16,128]{2,1,0:T(8,128)(2,1)S(1)} %collective-permute-done.7.refs_3_), channel_id=1, source_target_pairs={{0,1},{1,0},{2,3},{3,2},{4,5},{5,4},{6,7},{7,6},{8,9},{9,8},{10,11... | collective-permute-start | bytes 1769480 | tf_op jit(solution)/shard_map/ppermute | solution.py:430
  73.7 5.7 %collective-permute-start.15 = (bf16[144,16,128]{2,1,0:T(8,128)(2,1)S(1)}, bf16[144,16,128]{2,1,0:T(8,128)(2,1)S(1)}, u32[]{:S(2)}, u32[]{:S(2)}) collective-permute-start(bf16[144,16,128]{2,1,0:T(8,128)(2,1)S(1)} %collective-permute-done.8.refs_4_), channel_id=1, source_target_pairs={{0,1},{1,0},{2,3},{3,2},{4,5},{5,4},{6,7},{7,6},{8,9},{9,8},{10,11... | collective-permute-start | bytes 1769480 | tf_op jit(solution)/shard_map/ppermute | solution.py:430
  77.7 2.5 %collective-permute-start.16 = (bf16[144,16,128]{2,1,0:T(8,128)(2,1)S(1)}, bf16[144,16,128]{2,1,0:T(8,128)(2,1)S(1)}, u32[]{:S(2)}, u32[]{:S(2)}) collective-permute-start(bf16[144,16,128]{2,1,0:T(8,128)(2,1)S(1)} %collective-permute-done.9.refs_5_), channel_id=1, source_target_pairs={{0,1},{1,0},{2,3},{3,2},{4,5},{5,4},{6,7},{7,6},{8,9},{9,8},{10,11... | collective-permute-start | bytes 1769480 | tf_op jit(solution)/shard_map/ppermute | solution.py:430
  80.2 3.2 %collective-permute-start.17 = (bf16[144,16,128]{2,1,0:T(8,128)(2,1)S(1)}, bf16[144,16,128]{2,1,0:T(8,128)(2,1)S(1)}, u32[]{:S(2)}, u32[]{:S(2)}) collective-permute-start(bf16[144,16,128]{2,1,0:T(8,128)(2,1)S(1)} %collective-permute-done.10.refs_6_), channel_id=1, source_target_pairs={{0,1},{1,0},{2,3},{3,2},{4,5},{5,4},{6,7},{7,6},{8,9},{9,8},{10,11... | collective-permute-start | bytes 1769480 | tf_op jit(solution)/shard_map/ppermute | solution.py:430
  80.6 2.8 %collective-permute-start.18 = (bf16[144,16,128]{2,1,0:T(8,128)(2,1)S(1)}, bf16[144,16,128]{2,1,0:T(8,128)(2,1)S(1)}, u32[]{:S(2)}, u32[]{:S(2)}) collective-permute-start(bf16[144,16,128]{2,1,0:T(8,128)(2,1)S(1)} %collective-permute-done.11.refs_7_), channel_id=1, source_target_pairs={{0,1},{1,0},{2,3},{3,2},{4,5},{5,4},{6,7},{7,6},{8,9},{9,8},{10,11... | collective-permute-start | bytes 1769480 | tf_op jit(solution)/shard_map/ppermute | solution.py:430
  80.7 16.6 %collective-permute-start.19 = (bf16[4608,128]{1,0:T(8,128)(2,1)S(1)}, bf16[4608,128]{1,0:T(8,128)(2,1)S(1)}, u32[]{:S(2)}, u32[]{:S(2)}) collective-permute-start(bf16[4608,128]{1,0:T(8,128)(2,1)S(1)} %shard_map.76.refs_4_), channel_id=1, source_target_pairs={{0,8},{1,3},{2,10},{3,5},{4,12},{5,7},{6,14},{7,1},{8,16},{9,11},{... | collective-permute-start | bytes 3538952 | tf_op jit(solution)/shard_map/ppermute | solution.py:430
  80.9 16.3 %collective-permute-start.20 = (bf16[4608,128]{1,0:T(8,128)(2,1)S(1)}, bf16[4608,128]{1,0:T(8,128)(2,1)S(1)}, u32[]{:S(2)}, u32[]{:S(2)}) collective-permute-start(bf16[4608,128]{1,0:T(8,128)(2,1)S(1)} %shard_map.76.refs_4_), channel_id=1, source_target_pairs={{0,24},{1,7},{2,26},{3,1},{4,28},{5,3},{6,30},{7,5},{8,0},{9,15},{... | collective-permute-start | bytes 3538952 | tf_op jit(solution)/shard_map/ppermute | solution.py:430
  96.0 19.9 %copy-start.1 = (f32[147456]{0:T(1024)S(1)}, f32[147456]{0:T(1024)}, u32[]{:S(2)}) copy-start(f32[147456]{0:T(1024)} %param.6) | copy-start | bytes 1769476
  97.3 18.7 %collective-permute-start.21 = (bf16[12288,128]{1,0:T(8,128)(2,1)S(1)}, bf16[12288,128]{1,0:T(8,128)(2,1)S(1)}, u32[]{:S(2)}, u32[]{:S(2)}) collective-permute-start(bf16[12288,128]{1,0:T(8,128)(2,1)S(1)} %shard_map.79.refs_0_), channel_id=1, source_target_pairs={{0,1},{1,0},{2,3},{3,2},{4,5},{5,4},{6,7},{7,6},{8,9},{9,8},{10,11... | collective-permute-start | bytes 9437192 | tf_op jit(solution)/shard_map/ppermute | solution.py:430
  98.5 16.6 %collective-permute-start.22 = (bf16[4608,128]{1,0:T(8,128)(2,1)S(1)}, bf16[4608,128]{1,0:T(8,128)(2,1)S(1)}, u32[]{:S(2)}, u32[]{:S(2)}) collective-permute-start(bf16[4608,128]{1,0:T(8,128)(2,1)S(1)} %collective-permute-done.19.refs_5_), channel_id=1, source_target_pairs={{0,8},{1,3},{2,10},{3,5},{4,12},{5,7},{6,14},{7,1},{8,16},{9,11},{... | collective-permute-start | bytes 3538952 | tf_op jit(solution)/shard_map/ppermute | solution.py:430
  98.7 17.2 %collective-permute-start.24 = (bf16[4608,128]{1,0:T(8,128)(2,1)S(1)}, bf16[4608,128]{1,0:T(8,128)(2,1)S(1)}, u32[]{:S(2)}, u32[]{:S(2)}) collective-permute-start(bf16[4608,128]{1,0:T(8,128)(2,1)S(1)} %collective-permute-done.19.refs_5_), channel_id=1, source_target_pairs={{0,1},{1,0},{2,3},{3,2},{4,5},{5,4},{6,7},{7,6},{8,9},{9,8},{10,11... | collective-permute-start | bytes 3538952 | tf_op jit(solution)/shard_map/ppermute | solution.py:430
  99.1 16.8 %collective-permute-start.23 = (bf16[4608,128]{1,0:T(8,128)(2,1)S(1)}, bf16[4608,128]{1,0:T(8,128)(2,1)S(1)}, u32[]{:S(2)}, u32[]{:S(2)}) collective-permute-start(bf16[4608,128]{1,0:T(8,128)(2,1)S(1)} %shard_map.76.refs_4_), channel_id=1, source_target_pairs={{0,1},{1,0},{2,3},{3,2},{4,5},{5,4},{6,7},{7,6},{8,9},{9,8},{10,11... | collective-permute-start | bytes 3538952 | tf_op jit(solution)/shard_map/ppermute | solution.py:430
  99.2 16.7 %collective-permute-start.25 = (bf16[4608,128]{1,0:T(8,128)(2,1)S(1)}, bf16[4608,128]{1,0:T(8,128)(2,1)S(1)}, u32[]{:S(2)}, u32[]{:S(2)}) collective-permute-start(bf16[4608,128]{1,0:T(8,128)(2,1)S(1)} %collective-permute-done.20.refs_6_), channel_id=1, source_target_pairs={{0,1},{1,0},{2,3},{3,2},{4,5},{5,4},{6,7},{7,6},{8,9},{9,8},{10,11... | collective-permute-start | bytes 3538952 | tf_op jit(solution)/shard_map/ppermute | solution.py:430
  115.1 7.2 %collective-permute-start.26 = (bf16[4608,128]{1,0:T(8,128)(2,1)S(1)}, bf16[4608,128]{1,0:T(8,128)(2,1)S(1)}, u32[]{:S(2)}, u32[]{:S(2)}) collective-permute-start(bf16[4608,128]{1,0:T(8,128)(2,1)S(1)} %collective-permute-done.22.refs_7_), channel_id=1, source_target_pairs={{0,1},{1,0},{2,3},{3,2},{4,5},{5,4},{6,7},{7,6},{8,9},{9,8},{10,11... | collective-permute-start | bytes 3538952 | tf_op jit(solution)/shard_map/ppermute | solution.py:430
  (2 other events, 11.1 us)

commit v2 on v1

--- a/solution.py
+++ b/solution.py
@@ -94,6 +94,14 @@
         length = taken[0].shape[0]
         for i, ref in enumerate(taken):
             out[length * i : length * i + length] = ref[...]
+
+
+def join_masters_kernel(own, near, far, back, out, sems):
+    copy = pltpu.make_async_copy(own, out.at[pl.ds(0, SHARD_ROWS), :], sems.at[0])
+    copy.start()
+    for i, ref in enumerate((near, far, back)):
+        out[SHARD_ROWS * (i + 1) : SHARD_ROWS * (i + 2), :] = ref[...]
+    copy.wait()
 
 
 def look_kernel(info, sums, g_ref, m_ref, nm_ref, look_ref, scratch):
@@ -447,7 +455,14 @@
     masters = [narrow] + [send(narrow, first_route(step)) for step in (1, 2, 3)]
     sums = lax.all_to_all(sums, "shard", 0, 0)
     sums = jnp.broadcast_to(jnp.sum(sums, axis=0, keepdims=True), (8, 128))
-    (quad,) = joined(masters, 1)
+    quad = pl.pallas_call(
+        join_masters_kernel,
+        out_shape=jax.ShapeDtypeStruct((4 * SHARD_ROWS, 128), bf16),
+        in_specs=[HBM, VM, VM, VM],
+        out_specs=VM,
+        scratch_shapes=[pltpu.SemaphoreType.DMA((1,))],
+        compiler_params=params(56),
+    )(*masters)
     quad, sums = lax.optimization_barrier((quad, sums))
     sums = lax.all_to_all(sums, "group", 0, 0)
 

time: 124 us -> 128 us (1.032)
  Pallas kernels: 37.1 us -> 40.3 us
    pallas_call x0 -> x1, Pallas kernels: none -> 3.12 us  [on_device(): pl.pallas_call(join_masters_kernel, out_shape=jax.ShapeDtypeStruct((4 * S...]
where the time goes in v2:
time: 128 us
  starting transfers between devices  49.5 us (39%)
  Pallas kernels  40.3 us (31%)
  waiting for transfers between devices  34.9 us (27%)
  local copies, waits for them, and re-layouts  2.1 us (2%)
    ppermute x27, starting transfers between devices, send(): return lax.ppermute(block, 'shard', route)  35.1 us
    pallas_call x2, Pallas kernels, orthogonalized(): pl.pallas_call(lambda *refs: matrix_kernel(last, *refs), out_shape=jax.Sh...  25.1 us
    ppermute x27, waiting for transfers between devices, send(): return lax.ppermute(block, 'shard', route)  21.8 us
    all_to_all x1, starting transfers between devices, on_device(): sums = lax.all_to_all(sums, 'group', 0, 0)  8.19 us
    all_to_all x1, waiting for transfers between devices, on_device(): sums = lax.all_to_all(sums, 'shard', 0, 0)  6.79 us
    all_to_all x1, waiting for transfers between devices, on_device(): sums = lax.all_to_all(sums, 'group', 0, 0)  6.37 us
    pallas_call x1, Pallas kernels, on_device(): pl.pallas_call(finish_kernel, out_shape=(weights_shape, flat_shape, flat_...  6.3 us
    all_to_all x1, starting transfers between devices, on_device(): sums = lax.all_to_all(sums, 'shard', 0, 0)  6.26 us
  transfers between devices with their start and end apart: 29, of which 10 were waited for; matrix products, arithmetic and copies ran while one was open for 0% of the time, Pallas kernels for 25%

profile of v2, /device:TPU:1, one launch (start us, length us, event | category | flops | bytes accessed | tf_op | source)
XLA Modules:
  0.0 128.0 jit_solution(17881777485577380506)
XLA Ops:
  0.6 2.0 %shard_map.75 = (f32[32,128]{1,0:T(8,128)}, bf16[1152,128]{1,0:T(8,128)(2,1)}) custom-call(f32[1152,128]{1,0:T(8,128)} %bitcast.14, f32[1152,128]{1,0:T(8,128)} %bitcast.16), custom_call_target="tpu_custom_call" | custom-call | tf_op jit(solution)/shard_map/pallas_call | solution.py:440
  2.6 2.1 %collective-permute-start = (bf16[1152,128]{1,0:T(8,128)(2,1)}, bf16[1152,128]{1,0:T(8,128)(2,1)S(1)}, u32[]{:S(2)}, u32[]{:S(2)}) collective-permute-start(bf16[1152,128]{1,0:T(8,128)(2,1)} %get-tuple-element.35.own), channel_id=1, source_target_pairs={{0,2},{1,9},{2,4},{3,11},{4,6},{5,13},{6,0},{7,15},{8,10},{9,17},{... | collective-permute-start | bytes 884744 | tf_op jit(solution)/shard_map/ppermute | solution.py:438
  4.8 2.5 %collective-permute-start.1 = (bf16[1152,128]{1,0:T(8,128)(2,1)}, bf16[1152,128]{1,0:T(8,128)(2,1)S(1)}, u32[]{:S(2)}, u32[]{:S(2)}) collective-permute-start(bf16[1152,128]{1,0:T(8,128)(2,1)} %get-tuple-element.35.own), channel_id=1, source_target_pairs={{0,4},{1,17},{2,6},{3,19},{4,0},{5,21},{6,2},{7,23},{8,12},{9,25},... | collective-permute-start | bytes 884744 | tf_op jit(solution)/shard_map/ppermute | solution.py:438
  7.2 1.2 collective-permute-start.2
  8.4 6.3 %all-to-all-start = ((f32[32,1,128]{2,1,0:T(1,128)}), f32[32,1,128]{2,1,0:T(1,128)S(1)}, u32[]{:S(2)}, u32[]{:S(2)}) async-start(f32[32,1,128]{2,1,0:T(1,128)} %bitcast.21), calls=%async_computation | async-start | bytes 32768 | tf_op jit(solution)/shard_map/all_to_all | solution.py:456
  14.7 6.8 %all-to-all-done = f32[32,1,128]{2,1,0:T(1,128)S(1)} async-done(((f32[32,1,128]{2,1,0:T(1,128)}), f32[32,1,128]{2,1,0:T(1,128)S(1)}, u32[]{:S(2)}, u32[]{:S(2)}) %all-to-all-start) | async-done | bytes 16416 | tf_op jit(solution)/shard_map/all_to_all | solution.py:456
  23.1 3.1 %shard_map.76.refs_4_ = bf16[4608,128]{1,0:T(8,128)(2,1)} custom-call(bf16[1152,128]{1,0:T(8,128)(2,1)} %get-tuple-element.35.own, bf16[1152,128]{1,0:T(8,128)(2,1)} %copy-done.4, bf16[1152,128]{1,0:T(8,128)(2,1)} %copy-done.5, bf16[1152,128]{1,0:T(8,128)(2,1)} %copy-done.6), custom_call_target="tpu_custom_call" | custom-call | tf_op jit(solution)/shard_map/pallas_call | solution.py:458
  26.8 8.2 %all-to-all-start.1 = ((f32[8,1,128]{2,1,0:T(1,128)}), f32[8,1,128]{2,1,0:T(1,128)S(1)}, u32[]{:S(2)}, u32[]{:S(2)}) async-start(f32[8,1,128]{2,1,0:T(1,128)} %bitcast.6), calls=%async_computation.1 | async-start | bytes 8192 | tf_op jit(solution)/shard_map/all_to_all | solution.py:467
  35.1 6.4 %all-to-all-done.1 = f32[8,1,128]{2,1,0:T(1,128)S(1)} async-done(((f32[8,1,128]{2,1,0:T(1,128)}), f32[8,1,128]{2,1,0:T(1,128)S(1)}, u32[]{:S(2)}, u32[]{:S(2)}) %all-to-all-start.1) | async-done | bytes 4128 | tf_op jit(solution)/shard_map/all_to_all | solution.py:467
  41.5 1.9 %shard_map.77 = (f32[1152,128]{1,0:T(8,128)}, bf16[72,16,128]{2,1,0:T(8,128)(2,1)S(1)}) custom-call(s32[58]{0:T(128)S(1)} %pad_add_fusion.info.refs_0_, f32[8,128]{1,0:T(8,128)S(1)} %bitcast.19, f32[1152,128]{1,0:T(8,128)S(1)} %bitcast.15, f32[1152,128]{1,0:T(8,128)S(1)} %bitcast.18), custom_call_target="tpu_custom_call" | custom-call | tf_op jit(solution)/shard_map/pallas_call | solution.py:470
  43.7 1.6 %collective-permute-start.4 = (bf16[72,16,128]{2,1,0:T(8,128)(2,1)S(1)}, bf16[72,16,128]{2,1,0:T(8,128)(2,1)S(1)}, u32[]{:S(2)}, u32[]{:S(2)}) collective-permute-start(bf16[72,16,128]{2,1,0:T(8,128)(2,1)S(1)} %get-tuple-element.39.refs_0_), channel_id=1, source_target_pairs={{0,4},{1,17},{2,6},{3,19},{4,0},{5,21},{6,2},{7,23},{8,12},{9,25},... | collective-permute-start | bytes 884744 | tf_op jit(solution)/shard_map/ppermute | solution.py:438
  45.2 1.0 collective-permute-start.5
  46.2 7.3 %collective-permute-done.3.refs_1_ = bf16[72,16,128]{2,1,0:T(8,128)(2,1)S(1)} collective-permute-done((bf16[72,16,128]{2,1,0:T(8,128)(2,1)S(1)}, bf16[72,16,128]{2,1,0:T(8,128)(2,1)S(1)}, u32[]{:S(2)}, u32[]{:S(2)}) %collective-permute-start.3) | collective-permute-done | bytes 294944 | tf_op jit(solution)/shard_map/ppermute | solution.py:438
  54.7 2.4 %collective-permute-start.7 = (bf16[144,16,128]{2,1,0:T(8,128)(2,1)S(1)}, bf16[144,16,128]{2,1,0:T(8,128)(2,1)S(1)}, u32[]{:S(2)}, u32[]{:S(2)}) collective-permute-start(bf16[144,16,128]{2,1,0:T(8,128)(2,1)S(1)} %get-tuple-element.44), channel_id=1, source_target_pairs={{0,24},{1,7},{2,26},{3,1},{4,28},{5,3},{6,30},{7,5},{8,0},{9,15},{... | collective-permute-start | bytes 1769480 | tf_op jit(solution)/shard_map/ppermute | solution.py:438
  57.1 2.7 %collective-permute-start.9 = (bf16[144,16,128]{2,1,0:T(8,128)(2,1)S(1)}, bf16[144,16,128]{2,1,0:T(8,128)(2,1)S(1)}, u32[]{:S(2)}, u32[]{:S(2)}) collective-permute-start(bf16[144,16,128]{2,1,0:T(8,128)(2,1)S(1)} %get-tuple-element.41), channel_id=1, source_target_pairs={{0,24},{1,7},{2,26},{3,1},{4,28},{5,3},{6,30},{7,5},{8,0},{9,15},{... | collective-permute-start | bytes 1769480 | tf_op jit(solution)/shard_map/ppermute | solution.py:438
  59.8 4.9 %collective-permute-done.6.refs_2_ = bf16[144,16,128]{2,1,0:T(8,128)(2,1)S(1)} collective-permute-done((bf16[144,16,128]{2,1,0:T(8,128)(2,1)S(1)}, bf16[144,16,128]{2,1,0:T(8,128)(2,1)S(1)}, u32[]{:S(2)}, u32[]{:S(2)}) %collective-permute-start.6) | collective-permute-done | bytes 589856 | tf_op jit(solution)/shard_map/ppermute | solution.py:438
  64.7 2.7 %collective-permute-start.11 = (bf16[144,16,128]{2,1,0:T(8,128)(2,1)S(1)}, bf16[144,16,128]{2,1,0:T(8,128)(2,1)S(1)}, u32[]{:S(2)}, u32[]{:S(2)}) collective-permute-start(bf16[144,16,128]{2,1,0:T(8,128)(2,1)S(1)} %collective-permute-done.7.refs_3_), channel_id=1, source_target_pairs={{0,24},{1,7},{2,26},{3,1},{4,28},{5,3},{6,30},{7,5},{8,0},{9,15},{... | collective-permute-start | bytes 1769480 | tf_op jit(solution)/shard_map/ppermute | solution.py:438
  67.3 4.6 %collective-permute-start.12 = (bf16[288,16,128]{2,1,0:T(8,128)(2,1)S(1)}, bf16[288,16,128]{2,1,0:T(8,128)(2,1)S(1)}, u32[]{:S(2)}, u32[]{:S(2)}) collective-permute-start(bf16[288,16,128]{2,1,0:T(8,128)(2,1)S(1)} %get-tuple-element.42.refs_1_), channel_id=1, source_target_pairs={{0,1},{1,0},{2,3},{3,2},{4,5},{5,4},{6,7},{7,6},{8,9},{9,8},{10,11... | collective-permute-start | bytes 3538952 | tf_op jit(solution)/shard_map/ppermute | solution.py:438
  72.0 3.1 %collective-permute-start.13 = (bf16[144,16,128]{2,1,0:T(8,128)(2,1)S(1)}, bf16[144,16,128]{2,1,0:T(8,128)(2,1)S(1)}, u32[]{:S(2)}, u32[]{:S(2)}) collective-permute-start(bf16[144,16,128]{2,1,0:T(8,128)(2,1)S(1)} %collective-permute-done.6.refs_2_), channel_id=1, source_target_pairs={{0,1},{1,0},{2,3},{3,2},{4,5},{5,4},{6,7},{7,6},{8,9},{9,8},{10,11... | collective-permute-start | bytes 1769480 | tf_op jit(solution)/shard_map/ppermute | solution.py:438
  75.1 2.2 %collective-permute-done.10.refs_6_ = bf16[144,16,128]{2,1,0:T(8,128)(2,1)S(1)} collective-permute-done((bf16[144,16,128]{2,1,0:T(8,128)(2,1)S(1)}, bf16[144,16,128]{2,1,0:T(8,128)(2,1)S(1)}, u32[]{:S(2)}, u32[]{:S(2)}) %collective-permute-start.10) | collective-permute-done | bytes 589856 | tf_op jit(solution)/shard_map/ppermute | solution.py:438
  77.3 4.1 %collective-permute-start.15 = (bf16[144,16,128]{2,1,0:T(8,128)(2,1)S(1)}, bf16[144,16,128]{2,1,0:T(8,128)(2,1)S(1)}, u32[]{:S(2)}, u32[]{:S(2)}) collective-permute-start(bf16[144,16,128]{2,1,0:T(8,128)(2,1)S(1)} %collective-permute-done.8.refs_4_), channel_id=1, source_target_pairs={{0,1},{1,0},{2,3},{3,2},{4,5},{5,4},{6,7},{7,6},{8,9},{9,8},{10,11... | collective-permute-start | bytes 1769480 | tf_op jit(solution)/shard_map/ppermute | solution.py:438
  81.4 1.6 %collective-permute-done.15.refs_11_ = bf16[144,16,128]{2,1,0:T(8,128)(2,1)S(1)} collective-permute-done((bf16[144,16,128]{2,1,0:T(8,128)(2,1)S(1)}, bf16[144,16,128]{2,1,0:T(8,128)(2,1)S(1)}, u32[]{:S(2)}, u32[]{:S(2)}) %collective-permute-start.15) | collective-permute-done | bytes 589856 | tf_op jit(solution)/shard_map/ppermute | solution.py:438
  83.0 0.8 collective-permute-done.16.refs_12_
  84.6 2.4 %collective-permute-start.20 = (bf16[4608,128]{1,0:T(8,128)(2,1)S(1)}, bf16[4608,128]{1,0:T(8,128)(2,1)S(1)}, u32[]{:S(2)}, u32[]{:S(2)}) collective-permute-start(bf16[4608,128]{1,0:T(8,128)(2,1)S(1)} %copy-done), channel_id=1, source_target_pairs={{0,24},{1,7},{2,26},{3,1},{4,28},{5,3},{6,30},{7,5},{8,0},{9,15},{... | collective-permute-start | bytes 3538952 | tf_op jit(solution)/shard_map/ppermute | solution.py:438
  87.1 12.6 %shard_map.79.refs_0_ = bf16[12288,128]{1,0:T(8,128)(2,1)S(1)} custom-call(s32[58]{0:T(128)S(1)} %pad_add_fusion.info.refs_0_, bf16[288,16,128]{2,1,0:T(8,128)(2,1)S(1)} %get-tuple-element.42.refs_1_, bf16[144,16,128]{2,1,0:T(8,128)(2,1)S(1)} %collective-permute-done.6.refs_2_, bf16[144,16,128]{2,1,0:T(8,128)(2,1)S(1)} %collective-permute-done.7.refs_3_, ...), custom_call_target="tpu_custom_call" | custom-call | flops 9299999744 | bytes 20000000 | tf_op jit(solution)/shard_map/pallas_call | solution.py:494
  99.7 1.2 collective-permute-done.19.refs_5_
  100.9 1.2 collective-permute-start.21
  103.3 12.5 %shard_map.80.refs_2_ = bf16[12288,128]{1,0:T(8,128)(2,1)S(1)} custom-call(s32[58]{0:T(128)S(1)} %pad_add_fusion.info.refs_0_, bf16[288,16,128]{2,1,0:T(8,128)(2,1)S(1)} %get-tuple-element.42.refs_1_, bf16[144,16,128]{2,1,0:T(8,128)(2,1)S(1)} %collective-permute-done.6.refs_2_, bf16[144,16,128]{2,1,0:T(8,128)(2,1)S(1)} %collective-permute-done.7.refs_3_, ...), custom_call_target="tpu_custom_call" | custom-call | flops 9299999744 | bytes 20000000 | tf_op jit(solution)/shard_map/pallas_call | solution.py:494
  115.8 2.9 %collective-permute-done.22.refs_7_ = bf16[4608,128]{1,0:T(8,128)(2,1)S(1)} collective-permute-done((bf16[4608,128]{1,0:T(8,128)(2,1)S(1)}, bf16[4608,128]{1,0:T(8,128)(2,1)S(1)}, u32[]{:S(2)}, u32[]{:S(2)}) %collective-permute-start.22) | collective-permute-done | bytes 1179680 | tf_op jit(solution)/shard_map/ppermute | solution.py:438
  118.7 1.0 collective-permute-start.26
  119.8 6.3 %shard_map.81 = (bf16[36864,128]{1,0:T(8,128)(2,1)}, f32[1152,128]{1,0:T(8,128)}, f32[1152,128]{1,0:T(8,128)}, bf16[4608,128]{1,0:T(8,128)(2,1)S(1)}) custom-call(s32[58]{0:T(128)S(1)} %pad_add_fusion.info.refs_0_, bf16[12288,128]{1,0:T(8,128)(2,1)S(1)} %shard_map.79.refs_0_, bf16[12288,128]{1,0:T(8,128)(2,1)S(1)} %collective-permute-done.21.refs_1_, ...), custom_call_target="tpu_custom_call" | custom-call | flops 10000000 | bytes 28000000 | tf_op jit(solution)/shard_map/pallas_call | solution.py:514
  126.1 1.7 %shard_map.82 = bf16[36864,128]{1,0:T(8,128)(2,1)} custom-call(s32[58]{0:T(128)S(1)} %pad_add_fusion.info.refs_0_, bf16[36864,128]{1,0:T(8,128)(2,1)} %get-tuple-element.63._, bf16[4608,128]{1,0:T(8,128)(2,1)S(1)} %get-tuple-element.64.rest, bf16[4608,128]{1,0:T(8,128)(2,1)S(1)} %collective-permute-done.26.masters), custom_call_target="tpu_custom_call", output_to_operand_aliasing={{}: (1, {})} | custom-call | tf_op jit(solution)/shard_map/pallas_call | solution.py:528
  (54 shorter events, 5.6 us)
Async XLA Ops:
  2.6 18.9 %collective-permute-start = (bf16[1152,128]{1,0:T(8,128)(2,1)}, bf16[1152,128]{1,0:T(8,128)(2,1)S(1)}, u32[]{:S(2)}, u32[]{:S(2)}) collective-permute-start(bf16[1152,128]{1,0:T(8,128)(2,1)} %get-tuple-element.35.own), channel_id=1, source_target_pairs={{0,2},{1,9},{2,4},{3,11},{4,6},{5,13},{6,0},{7,15},{8,10},{9,17},{... | collective-permute-start | bytes 884744 | tf_op jit(solution)/shard_map/ppermute | solution.py:438
  4.8 16.8 %collective-permute-start.1 = (bf16[1152,128]{1,0:T(8,128)(2,1)}, bf16[1152,128]{1,0:T(8,128)(2,1)S(1)}, u32[]{:S(2)}, u32[]{:S(2)}) collective-permute-start(bf16[1152,128]{1,0:T(8,128)(2,1)} %get-tuple-element.35.own), channel_id=1, source_target_pairs={{0,4},{1,17},{2,6},{3,19},{4,0},{5,21},{6,2},{7,23},{8,12},{9,25},... | collective-permute-start | bytes 884744 | tf_op jit(solution)/shard_map/ppermute | solution.py:438
  7.2 14.4 %collective-permute-start.2 = (bf16[1152,128]{1,0:T(8,128)(2,1)}, bf16[1152,128]{1,0:T(8,128)(2,1)S(1)}, u32[]{:S(2)}, u32[]{:S(2)}) collective-permute-start(bf16[1152,128]{1,0:T(8,128)(2,1)} %get-tuple-element.35.own), channel_id=1, source_target_pairs={{0,6},{1,25},{2,0},{3,27},{4,2},{5,29},{6,4},{7,31},{8,14},{9,1},{... | collective-permute-start | bytes 884744 | tf_op jit(solution)/shard_map/ppermute | solution.py:438
  8.4 13.1 %all-to-all-start = ((f32[32,1,128]{2,1,0:T(1,128)}), f32[32,1,128]{2,1,0:T(1,128)S(1)}, u32[]{:S(2)}, u32[]{:S(2)}) async-start(f32[32,1,128]{2,1,0:T(1,128)} %bitcast.21), calls=%async_computation | async-start | bytes 32768 | tf_op jit(solution)/shard_map/all_to_all | solution.py:456
  21.5 19.9 %copy-start.1 = (f32[147456]{0:T(1024)S(1)}, f32[147456]{0:T(1024)}, u32[]{:S(2)}) copy-start(f32[147456]{0:T(1024)} %param.4) | copy-start | bytes 1769476
  26.8 14.6 %all-to-all-start.1 = ((f32[8,1,128]{2,1,0:T(1,128)}), f32[8,1,128]{2,1,0:T(1,128)S(1)}, u32[]{:S(2)}, u32[]{:S(2)}) async-start(f32[8,1,128]{2,1,0:T(1,128)} %bitcast.6), calls=%async_computation.1 | async-start | bytes 8192 | tf_op jit(solution)/shard_map/all_to_all | solution.py:467
  41.5 42.9 %copy-start = (bf16[4608,128]{1,0:T(8,128)(2,1)S(1)}, bf16[4608,128]{1,0:T(8,128)(2,1)}, u32[]{:S(2)}) copy-start(bf16[4608,128]{1,0:T(8,128)(2,1)} %shard_map.76.refs_4_) | copy-start | bytes 3538948
  43.3 10.2 %collective-permute-start.3 = (bf16[72,16,128]{2,1,0:T(8,128)(2,1)S(1)}, bf16[72,16,128]{2,1,0:T(8,128)(2,1)S(1)}, u32[]{:S(2)}, u32[]{:S(2)}) collective-permute-start(bf16[72,16,128]{2,1,0:T(8,128)(2,1)S(1)} %get-tuple-element.39.refs_0_), channel_id=1, source_target_pairs={{0,2},{1,9},{2,4},{3,11},{4,6},{5,13},{6,0},{7,15},{8,10},{9,17},{... | collective-permute-start | bytes 884744 | tf_op jit(solution)/shard_map/ppermute | solution.py:438
  43.7 9.9 %collective-permute-start.4 = (bf16[72,16,128]{2,1,0:T(8,128)(2,1)S(1)}, bf16[72,16,128]{2,1,0:T(8,128)(2,1)S(1)}, u32[]{:S(2)}, u32[]{:S(2)}) collective-permute-start(bf16[72,16,128]{2,1,0:T(8,128)(2,1)S(1)} %get-tuple-element.39.refs_0_), channel_id=1, source_target_pairs={{0,4},{1,17},{2,6},{3,19},{4,0},{5,21},{6,2},{7,23},{8,12},{9,25},... | collective-permute-start | bytes 884744 | tf_op jit(solution)/shard_map/ppermute | solution.py:438
  45.2 8.9 %collective-permute-start.5 = (bf16[72,16,128]{2,1,0:T(8,128)(2,1)S(1)}, bf16[72,16,128]{2,1,0:T(8,128)(2,1)S(1)}, u32[]{:S(2)}, u32[]{:S(2)}) collective-permute-start(bf16[72,16,128]{2,1,0:T(8,128)(2,1)S(1)} %get-tuple-element.39.refs_0_), channel_id=1, source_target_pairs={{0,6},{1,25},{2,0},{3,27},{4,2},{5,29},{6,4},{7,31},{8,14},{9,1},{... | collective-permute-start | bytes 884744 | tf_op jit(solution)/shard_map/ppermute | solution.py:438
  54.4 10.3 %collective-permute-start.6 = (bf16[144,16,128]{2,1,0:T(8,128)(2,1)S(1)}, bf16[144,16,128]{2,1,0:T(8,128)(2,1)S(1)}, u32[]{:S(2)}, u32[]{:S(2)}) collective-permute-start(bf16[144,16,128]{2,1,0:T(8,128)(2,1)S(1)} %get-tuple-element.41), channel_id=1, source_target_pairs={{0,8},{1,3},{2,10},{3,5},{4,12},{5,7},{6,14},{7,1},{8,16},{9,11},{... | collective-permute-start | bytes 1769480 | tf_op jit(solution)/shard_map/ppermute | solution.py:438
  54.7 10.0 %collective-permute-start.7 = (bf16[144,16,128]{2,1,0:T(8,128)(2,1)S(1)}, bf16[144,16,128]{2,1,0:T(8,128)(2,1)S(1)}, u32[]{:S(2)}, u32[]{:S(2)}) collective-permute-start(bf16[144,16,128]{2,1,0:T(8,128)(2,1)S(1)} %get-tuple-element.44), channel_id=1, source_target_pairs={{0,24},{1,7},{2,26},{3,1},{4,28},{5,3},{6,30},{7,5},{8,0},{9,15},{... | collective-permute-start | bytes 1769480 | tf_op jit(solution)/shard_map/ppermute | solution.py:438
  57.1 14.9 %collective-permute-start.8 = (bf16[144,16,128]{2,1,0:T(8,128)(2,1)S(1)}, bf16[144,16,128]{2,1,0:T(8,128)(2,1)S(1)}, u32[]{:S(2)}, u32[]{:S(2)}) collective-permute-start(bf16[144,16,128]{2,1,0:T(8,128)(2,1)S(1)} %get-tuple-element.44), channel_id=1, source_target_pairs={{0,8},{1,3},{2,10},{3,5},{4,12},{5,7},{6,14},{7,1},{8,16},{9,11},{... | collective-permute-start | bytes 1769480 | tf_op jit(solution)/shard_map/ppermute | solution.py:438
  57.1 18.0 %collective-permute-start.9 = (bf16[144,16,128]{2,1,0:T(8,128)(2,1)S(1)}, bf16[144,16,128]{2,1,0:T(8,128)(2,1)S(1)}, u32[]{:S(2)}, u32[]{:S(2)}) collective-permute-start(bf16[144,16,128]{2,1,0:T(8,128)(2,1)S(1)} %get-tuple-element.41), channel_id=1, source_target_pairs={{0,24},{1,7},{2,26},{3,1},{4,28},{5,3},{6,30},{7,5},{8,0},{9,15},{... | collective-permute-start | bytes 1769480 | tf_op jit(solution)/shard_map/ppermute | solution.py:438
  64.7 12.6 %collective-permute-start.10 = (bf16[144,16,128]{2,1,0:T(8,128)(2,1)S(1)}, bf16[144,16,128]{2,1,0:T(8,128)(2,1)S(1)}, u32[]{:S(2)}, u32[]{:S(2)}) collective-permute-start(bf16[144,16,128]{2,1,0:T(8,128)(2,1)S(1)} %collective-permute-done.6.refs_2_), channel_id=1, source_target_pairs={{0,8},{1,3},{2,10},{3,5},{4,12},{5,7},{6,14},{7,1},{8,16},{9,11},{... | collective-permute-start | bytes 1769480 | tf_op jit(solution)/shard_map/ppermute | solution.py:438
  64.7 16.7 %collective-permute-start.11 = (bf16[144,16,128]{2,1,0:T(8,128)(2,1)S(1)}, bf16[144,16,128]{2,1,0:T(8,128)(2,1)S(1)}, u32[]{:S(2)}, u32[]{:S(2)}) collective-permute-start(bf16[144,16,128]{2,1,0:T(8,128)(2,1)S(1)} %collective-permute-done.7.refs_3_), channel_id=1, source_target_pairs={{0,24},{1,7},{2,26},{3,1},{4,28},{5,3},{6,30},{7,5},{8,0},{9,15},{... | collective-permute-start | bytes 1769480 | tf_op jit(solution)/shard_map/ppermute | solution.py:438
  67.3 16.5 %collective-permute-start.12 = (bf16[288,16,128]{2,1,0:T(8,128)(2,1)S(1)}, bf16[288,16,128]{2,1,0:T(8,128)(2,1)S(1)}, u32[]{:S(2)}, u32[]{:S(2)}) collective-permute-start(bf16[288,16,128]{2,1,0:T(8,128)(2,1)S(1)} %get-tuple-element.42.refs_1_), channel_id=1, source_target_pairs={{0,1},{1,0},{2,3},{3,2},{4,5},{5,4},{6,7},{7,6},{8,9},{9,8},{10,11... | collective-permute-start | bytes 3538952 | tf_op jit(solution)/shard_map/ppermute | solution.py:438
  72.0 9.4 %collective-permute-start.13 = (bf16[144,16,128]{2,1,0:T(8,128)(2,1)S(1)}, bf16[144,16,128]{2,1,0:T(8,128)(2,1)S(1)}, u32[]{:S(2)}, u32[]{:S(2)}) collective-permute-start(bf16[144,16,128]{2,1,0:T(8,128)(2,1)S(1)} %collective-permute-done.6.refs_2_), channel_id=1, source_target_pairs={{0,1},{1,0},{2,3},{3,2},{4,5},{5,4},{6,7},{7,6},{8,9},{9,8},{10,11... | collective-permute-start | bytes 1769480 | tf_op jit(solution)/shard_map/ppermute | solution.py:438
  75.1 6.3 %collective-permute-start.14 = (bf16[144,16,128]{2,1,0:T(8,128)(2,1)S(1)}, bf16[144,16,128]{2,1,0:T(8,128)(2,1)S(1)}, u32[]{:S(2)}, u32[]{:S(2)}) collective-permute-start(bf16[144,16,128]{2,1,0:T(8,128)(2,1)S(1)} %collective-permute-done.7.refs_3_), channel_id=1, source_target_pairs={{0,1},{1,0},{2,3},{3,2},{4,5},{5,4},{6,7},{7,6},{8,9},{9,8},{10,11... | collective-permute-start | bytes 1769480 | tf_op jit(solution)/shard_map/ppermute | solution.py:438
  77.3 5.7 %collective-permute-start.15 = (bf16[144,16,128]{2,1,0:T(8,128)(2,1)S(1)}, bf16[144,16,128]{2,1,0:T(8,128)(2,1)S(1)}, u32[]{:S(2)}, u32[]{:S(2)}) collective-permute-start(bf16[144,16,128]{2,1,0:T(8,128)(2,1)S(1)} %collective-permute-done.8.refs_4_), channel_id=1, source_target_pairs={{0,1},{1,0},{2,3},{3,2},{4,5},{5,4},{6,7},{7,6},{8,9},{9,8},{10,11... | collective-permute-start | bytes 1769480 | tf_op jit(solution)/shard_map/ppermute | solution.py:438
  81.4 2.5 %collective-permute-start.16 = (bf16[144,16,128]{2,1,0:T(8,128)(2,1)S(1)}, bf16[144,16,128]{2,1,0:T(8,128)(2,1)S(1)}, u32[]{:S(2)}, u32[]{:S(2)}) collective-permute-start(bf16[144,16,128]{2,1,0:T(8,128)(2,1)S(1)} %collective-permute-done.9.refs_5_), channel_id=1, source_target_pairs={{0,1},{1,0},{2,3},{3,2},{4,5},{5,4},{6,7},{7,6},{8,9},{9,8},{10,11... | collective-permute-start | bytes 1769480 | tf_op jit(solution)/shard_map/ppermute | solution.py:438
  83.9 3.2 %collective-permute-start.17 = (bf16[144,16,128]{2,1,0:T(8,128)(2,1)S(1)}, bf16[144,16,128]{2,1,0:T(8,128)(2,1)S(1)}, u32[]{:S(2)}, u32[]{:S(2)}) collective-permute-start(bf16[144,16,128]{2,1,0:T(8,128)(2,1)S(1)} %collective-permute-done.10.refs_6_), channel_id=1, source_target_pairs={{0,1},{1,0},{2,3},{3,2},{4,5},{5,4},{6,7},{7,6},{8,9},{9,8},{10,11... | collective-permute-start | bytes 1769480 | tf_op jit(solution)/shard_map/ppermute | solution.py:438
  84.2 2.8 %collective-permute-start.18 = (bf16[144,16,128]{2,1,0:T(8,128)(2,1)S(1)}, bf16[144,16,128]{2,1,0:T(8,128)(2,1)S(1)}, u32[]{:S(2)}, u32[]{:S(2)}) collective-permute-start(bf16[144,16,128]{2,1,0:T(8,128)(2,1)S(1)} %collective-permute-done.11.refs_7_), channel_id=1, source_target_pairs={{0,1},{1,0},{2,3},{3,2},{4,5},{5,4},{6,7},{7,6},{8,9},{9,8},{10,11... | collective-permute-start | bytes 1769480 | tf_op jit(solution)/shard_map/ppermute | solution.py:438
  84.4 16.6 %collective-permute-start.19 = (bf16[4608,128]{1,0:T(8,128)(2,1)S(1)}, bf16[4608,128]{1,0:T(8,128)(2,1)S(1)}, u32[]{:S(2)}, u32[]{:S(2)}) collective-permute-start(bf16[4608,128]{1,0:T(8,128)(2,1)S(1)} %copy-done), channel_id=1, source_target_pairs={{0,8},{1,3},{2,10},{3,5},{4,12},{5,7},{6,14},{7,1},{8,16},{9,11},{... | collective-permute-start | bytes 3538952 | tf_op jit(solution)/shard_map/ppermute | solution.py:438
  84.6 16.3 %collective-permute-start.20 = (bf16[4608,128]{1,0:T(8,128)(2,1)S(1)}, bf16[4608,128]{1,0:T(8,128)(2,1)S(1)}, u32[]{:S(2)}, u32[]{:S(2)}) collective-permute-start(bf16[4608,128]{1,0:T(8,128)(2,1)S(1)} %copy-done), channel_id=1, source_target_pairs={{0,24},{1,7},{2,26},{3,1},{4,28},{5,3},{6,30},{7,5},{8,0},{9,15},{... | collective-permute-start | bytes 3538952 | tf_op jit(solution)/shard_map/ppermute | solution.py:438
  99.7 20.1 %copy-start.2 = (f32[147456]{0:T(1024)S(1)}, f32[147456]{0:T(1024)}, u32[]{:S(2)}) copy-start(f32[147456]{0:T(1024)} %param.6) | copy-start | bytes 1769476
  100.9 18.8 %collective-permute-start.21 = (bf16[12288,128]{1,0:T(8,128)(2,1)S(1)}, bf16[12288,128]{1,0:T(8,128)(2,1)S(1)}, u32[]{:S(2)}, u32[]{:S(2)}) collective-permute-start(bf16[12288,128]{1,0:T(8,128)(2,1)S(1)} %shard_map.79.refs_0_), channel_id=1, source_target_pairs={{0,1},{1,0},{2,3},{3,2},{4,5},{5,4},{6,7},{7,6},{8,9},{9,8},{10,11... | collective-permute-start | bytes 9437192 | tf_op jit(solution)/shard_map/ppermute | solution.py:438
  102.2 16.6 %collective-permute-start.22 = (bf16[4608,128]{1,0:T(8,128)(2,1)S(1)}, bf16[4608,128]{1,0:T(8,128)(2,1)S(1)}, u32[]{:S(2)}, u32[]{:S(2)}) collective-permute-start(bf16[4608,128]{1,0:T(8,128)(2,1)S(1)} %collective-permute-done.19.refs_5_), channel_id=1, source_target_pairs={{0,8},{1,3},{2,10},{3,5},{4,12},{5,7},{6,14},{7,1},{8,16},{9,11},{... | collective-permute-start | bytes 3538952 | tf_op jit(solution)/shard_map/ppermute | solution.py:438
  102.4 17.4 %collective-permute-start.24 = (bf16[4608,128]{1,0:T(8,128)(2,1)S(1)}, bf16[4608,128]{1,0:T(8,128)(2,1)S(1)}, u32[]{:S(2)}, u32[]{:S(2)}) collective-permute-start(bf16[4608,128]{1,0:T(8,128)(2,1)S(1)} %collective-permute-done.19.refs_5_), channel_id=1, source_target_pairs={{0,1},{1,0},{2,3},{3,2},{4,5},{5,4},{6,7},{7,6},{8,9},{9,8},{10,11... | collective-permute-start | bytes 3538952 | tf_op jit(solution)/shard_map/ppermute | solution.py:438
  102.7 17.0 %collective-permute-start.23 = (bf16[4608,128]{1,0:T(8,128)(2,1)S(1)}, bf16[4608,128]{1,0:T(8,128)(2,1)S(1)}, u32[]{:S(2)}, u32[]{:S(2)}) collective-permute-start(bf16[4608,128]{1,0:T(8,128)(2,1)S(1)} %copy-done), channel_id=1, source_target_pairs={{0,1},{1,0},{2,3},{3,2},{4,5},{5,4},{6,7},{7,6},{8,9},{9,8},{10,11... | collective-permute-start | bytes 3538952 | tf_op jit(solution)/shard_map/ppermute | solution.py:438
  102.9 16.9 %collective-permute-start.25 = (bf16[4608,128]{1,0:T(8,128)(2,1)S(1)}, bf16[4608,128]{1,0:T(8,128)(2,1)S(1)}, u32[]{:S(2)}, u32[]{:S(2)}) collective-permute-start(bf16[4608,128]{1,0:T(8,128)(2,1)S(1)} %collective-permute-done.20.refs_6_), channel_id=1, source_target_pairs={{0,1},{1,0},{2,3},{3,2},{4,5},{5,4},{6,7},{7,6},{8,9},{9,8},{10,11... | collective-permute-start | bytes 3538952 | tf_op jit(solution)/shard_map/ppermute | solution.py:438
  118.7 7.4 %collective-permute-start.26 = (bf16[4608,128]{1,0:T(8,128)(2,1)S(1)}, bf16[4608,128]{1,0:T(8,128)(2,1)S(1)}, u32[]{:S(2)}, u32[]{:S(2)}) collective-permute-start(bf16[4608,128]{1,0:T(8,128)(2,1)S(1)} %collective-permute-done.22.refs_7_), channel_id=1, source_target_pairs={{0,1},{1,0},{2,3},{3,2},{4,5},{5,4},{6,7},{7,6},{8,9},{9,8},{10,11... | collective-permute-start | bytes 3538952 | tf_op jit(solution)/shard_map/ppermute | solution.py:438
  (5 other events, 35.6 us)
